TPU v7x, 128 devices: a whole 4x4x4 slice. The times are simulated.
128 devices in a mesh: gx: 4 (over y), gy: 4 (over z), gz: 8 (over x, core).
Axes of the slice: x: 4, y: 4, z: 4, core: 2. Of those that a mesh axis runs over, the one named last changes fastest.
Arguments:
- position: float32 [16384, 3, 128], P(('gx', 'gy', 'gz')), may hold values from 0 to 8, as said below
- velocity: float32 [16384, 3, 128], P(('gx', 'gy', 'gz')), may hold values from -0.3 to 0.3
- particle_mass: float32 [16384, 128], P(('gx', 'gy', 'gz')), may hold values from 0.001953125 to 0.0078125
- send_first: int32 [128, 128, 4], P(('gx', 'gy', 'gz')), may hold values from -1 to 127, as said below
- neighbours_first: int32 [16384, 16], P(('gx', 'gy', 'gz')), may hold values from 0 to 639, as said below
- destination: int32 [16384], P(('gx', 'gy', 'gz')), may hold values from 0 to 16383, as said below
- send_second: int32 [128, 128, 4], P(('gx', 'gy', 'gz')), may hold values from -1 to 127, as said below
- neighbours_second: int32 [16384, 16], P(('gx', 'gy', 'gz')), may hold values from 0 to 639, as said below
Outputs:
- position_out: float32 [16384, 3, 128], P(('gx', 'gy', 'gz'))
- velocity_out: float32 [16384, 3, 128], P(('gx', 'gy', 'gz'))
- density_out: float32 [16384, 128], P(('gx', 'gy', 'gz'))
Inputs may be any that keep to these rules, and one draw needn't show every extreme that they name: The particles of a block owned by the device at grid position (i_gx, i_gy, i_gz) lie in its box [i_gx, i_gx + 1] x [i_gy, i_gy + 1] x [i_gz, i_gz + 1], all of one block within a cube of side 1/2. `send_first`: only devices whose grid positions along gx, gy and gz differ by at most one in each (and are not the same) send ghosts to each other. The filled slots of one pair come first and hold distinct blocks; some pair fills all 4 slots. `send_second`: as for send_first, in the new layout. `neighbours_first`: entries name only the device's own blocks or filled ghost slots of send_first; the entries of a block are distinct and never the block itself. `neighbours_second`: entries name only the device's own blocks or filled ghost slots of send_second; the entries of a block are distinct and never the block itself. `destination`: A permutation of the 16384 positions; a block stays or moves to a device next to its owner along exactly one of gx, gy, gz; at most 2 blocks go from one device to another, and some pairs move exactly 2.
All inputs are finite; a program needn't handle non-finite values.
Results may differ from a plain program's by a relative error of at most 0.0001.
Values sent between devices are 32-bit elements; how exact they have to be, the bound alone decides.
No kernel may reach another device: no remote copies, remote signals or barrier semaphores. Data moves between devices by JAX's collectives and lax.ppermute only.
A program may use at most 128 MiB of HBM per device.

v0:
```python
import jax
import jax.numpy as jnp
import numpy as np
from jax import lax
from jax.sharding import PartitionSpec as P

MOVE_CAP = 2


smooth_len = 0.5
time_step = 0.25
column_group = 4


def padded_2(block, sides, width):
    for axis, dim in sides:
        count = lax.axis_size(axis)
        forward = [(i, i + 1) for i in range(count - 1)]
        backward = [(target, source) for source, target in forward]
        low = lax.ppermute(
            lax.slice_in_dim(block, block.shape[dim] - width, None, axis=dim), axis, forward
        )
        high = lax.ppermute(lax.slice_in_dim(block, 0, width, axis=dim), axis, backward)
        block = jnp.concatenate([low, block, high], axis=dim)
    return block


def pair_density(home_points, away_points, away_mass):
    offset = home_points[:, :, :, None] - away_points[:, :, None, :]
    squared = jnp.sum(offset * offset, axis=1)
    kernel = jnp.maximum(1.0 - squared / (smooth_len * smooth_len), 0.0)
    return jnp.sum(away_mass[:, None, :] * (kernel * kernel * kernel), axis=2)


def pair_force(home_points, home_term, away_points, away_mass, away_term):
    offset = home_points[:, :, :, None] - away_points[:, :, None, :]
    squared = jnp.sum(offset * offset, axis=1)
    kernel = jnp.maximum(1.0 - squared / (smooth_len * smooth_len), 0.0)
    weight = (
        away_mass[:, None, :] * (home_term[:, :, None] + away_term[:, None, :]) * kernel * kernel
    )
    return 6.0 / (smooth_len * smooth_len) * jnp.sum(weight[:, None, :, :] * offset, axis=3)


def pressure_term(density):
    return jnp.exp(jnp.log(density) * (-1.0 / 3.0))


def joined_points(all_points, picked):
    chosen = all_points[picked]
    rows = chosen.shape[0]
    return jnp.transpose(chosen, (0, 2, 1, 3)).reshape(
        rows, chosen.shape[2], chosen.shape[1] * chosen.shape[3]
    )


def joined_values(all_values, picked):
    chosen = all_values[picked]
    return chosen.reshape(chosen.shape[0], chosen.shape[1] * chosen.shape[2])


def table_density(home_points, home_mass, all_points, all_mass, lookup):
    initial = pair_density(home_points, home_points, home_mass)

    def add_group(group, running):
        picked = lax.dynamic_slice_in_dim(lookup, group * column_group, column_group, 1)
        return running + pair_density(
            home_points, joined_points(all_points, picked), joined_values(all_mass, picked)
        )

    return lax.fori_loop(0, lookup.shape[1] // column_group, add_group, initial)


def table_force(home_points, home_mass, home_term, all_points, all_mass, all_term, lookup):
    initial = pair_force(home_points, home_term, home_points, home_mass, home_term)

    def add_group(group, running):
        picked = lax.dynamic_slice_in_dim(lookup, group * column_group, column_group, 1)
        return running + pair_force(
            home_points,
            home_term,
            joined_points(all_points, picked),
            joined_values(all_mass, picked),
            joined_values(all_term, picked),
        )

    return lax.fori_loop(0, lookup.shape[1] // column_group, add_group, initial)


def near_slots(sender_rows):
    size_x = lax.axis_size("gx")
    size_y = lax.axis_size("gy")
    size_z = lax.axis_size("gz")
    shifts = np.array(
        [
            [first, second, third]
            for first in (-1, 0, 1)
            for second in (-1, 0, 1)
            for third in (-1, 0, 1)
        ],
        dtype=np.int32,
    )
    target_x = lax.axis_index("gx") + shifts[:, 0]
    target_y = lax.axis_index("gy") + shifts[:, 1]
    target_z = lax.axis_index("gz") + shifts[:, 2]
    inside = (target_x >= 0) & (target_x < size_x) & (target_y >= 0) & (target_y < size_y)
    inside = inside & (target_z >= 0) & (target_z < size_z)
    target = (target_x * size_y + target_y) * size_z + target_z
    picked = sender_rows[jnp.clip(target, 0, sender_rows.shape[0] - 1)]
    return jnp.where(inside[:, None], picked, -1)


def fill_slots(payload, sender_rows, blank):
    usable = sender_rows >= 0
    gathered = payload[jnp.maximum(sender_rows, 0)]
    broadcast_shape = usable.shape + (1,) * (payload.ndim - 1)
    return jnp.where(usable.reshape(broadcast_shape), gathered, blank)


def ghost_blocks(payload, sender_rows):
    buffer = fill_slots(payload, near_slots(sender_rows), 0.0)
    cube = buffer.reshape((3, 3, 3) + buffer.shape[1:])
    padded = padded_2(cube, (("gx", 0), ("gy", 1), ("gz", 2)), 1)
    return padded[0::2, 0::2, 0::2].reshape((-1,) + payload.shape[1:])


def ghost_density(density, sender_rows):
    buffer = fill_slots(density, near_slots(sender_rows), 1.0)
    cube = buffer.reshape((3, 3, 3) + buffer.shape[1:])
    padded = padded_2(cube, (("gx", 0), ("gy", 1), ("gz", 2)), 1)
    return padded[0::2, 0::2, 0::2].reshape((-1,) + density.shape[1:])


def table_rows(neighbours, blocks, ghost_cap):
    size_y = lax.axis_size("gy")
    size_z = lax.axis_size("gz")
    remote = jnp.maximum(neighbours - blocks, 0)
    source = remote // ghost_cap
    within = remote % ghost_cap
    code = (source // (size_y * size_z) - lax.axis_index("gx") + 1) * 9
    code = code + (source // size_z % size_y - lax.axis_index("gy") + 1) * 3
    code = code + (source % size_z - lax.axis_index("gz") + 1)
    return jnp.where(neighbours < blocks, neighbours, blocks + code * ghost_cap + within)


def sph_forces(points, weights, sender_rows, neighbours):
    blocks = points.shape[0]
    payload = jnp.concatenate([points, weights[:, None, :]], axis=1)
    stacked = jnp.concatenate([payload, ghost_blocks(payload, sender_rows)], axis=0)
    lookup = table_rows(neighbours, blocks, sender_rows.shape[1])
    all_points = stacked[:, 0:3]
    all_mass = stacked[:, 3]
    density = table_density(points, weights, all_points, all_mass, lookup)
    all_rho = jnp.concatenate([density, ghost_density(density, sender_rows)], axis=0)
    all_term = pressure_term(all_rho)
    acceleration = table_force(
        points, weights, all_term[:blocks], all_points, all_mass, all_term, lookup
    )
    return (density, acceleration)


def migrate(fields, destination):
    blocks = fields.shape[0]
    width = fields.shape[2]
    myself = lax.axis_index(("gx", "gy", "gz"))
    owner_device = destination // blocks
    new_place = destination % blocks
    moving = owner_device != myself
    label_row = (
        jnp.zeros((blocks, 1, width), jnp.float32)
        .at[:, 0, 0]
        .set((new_place + 1).astype(jnp.float32))
    )
    carried = jnp.concatenate([fields, label_row], axis=1)
    staying = (
        jnp.zeros_like(fields).at[jnp.where(moving, blocks, new_place)].set(fields, mode="drop")
    )
    size_y = lax.axis_size("gy")
    size_z = lax.axis_size("gz")
    delta_x = owner_device // (size_y * size_z) - lax.axis_index("gx")
    delta_y = owner_device // size_z % size_y - lax.axis_index("gy")
    delta_z = owner_device % size_z - lax.axis_index("gz")
    heading = jnp.where(
        delta_x != 0,
        (delta_x > 0).astype(jnp.int32),
        jnp.where(
            delta_y != 0, 2 + (delta_y > 0).astype(jnp.int32), 4 + (delta_z > 0).astype(jnp.int32)
        ),
    )
    bin_count = 6
    onehot = (
        (heading[:, None] == jnp.arange(bin_count, dtype=jnp.int32)[None, :]) & moving[:, None]
    ).astype(jnp.int32)
    earlier = jnp.sum((jnp.cumsum(onehot, axis=0) - onehot) * onehot, axis=1)
    outbox_slot = jnp.where(moving, heading * MOVE_CAP + earlier, bin_count * MOVE_CAP)
    outbox = (
        jnp.zeros((bin_count * MOVE_CAP,) + carried.shape[1:], jnp.float32)
        .at[outbox_slot]
        .set(carried, mode="drop")
    )
    outbound = outbox.reshape((3, 2, MOVE_CAP) + carried.shape[1:])
    came_x = padded_2(outbound[0], (("gx", 0),), 1)
    came_y = padded_2(outbound[1], (("gy", 0),), 1)
    came_z = padded_2(outbound[2], (("gz", 0),), 1)
    arrived = jnp.concatenate(
        [came_x[0], came_x[3], came_y[0], came_y[3], came_z[0], came_z[3]], axis=0
    )
    labels = arrived[:, 7, 0]
    arrive_place = jnp.where(labels > 0.5, labels.astype(jnp.int32) - 1, blocks)
    return staying.at[arrive_place].set(arrived[:, 0:7], mode="drop")


def per_device(
    position,
    velocity,
    particle_mass,
    send_first,
    neighbours_first,
    destination,
    send_second,
    neighbours_second,
):
    density, acceleration = sph_forces(position, particle_mass, send_first[0], neighbours_first)
    velocity = velocity + time_step * acceleration
    position = position + time_step * velocity
    fields = jnp.concatenate([position, velocity, particle_mass[:, None, :]], axis=1)
    shifted = migrate(fields, destination)
    position = shifted[:, 0:3]
    velocity = shifted[:, 3:6]
    moved_mass = shifted[:, 6]
    density, acceleration = sph_forces(position, moved_mass, send_second[0], neighbours_second)
    velocity = velocity + time_step * acceleration
    position = position + time_step * velocity
    return (position, velocity, density)


def solution(mesh):
    in_specs = (
        P(("gx", "gy", "gz"), None, None),
        P(("gx", "gy", "gz"), None, None),
        P(("gx", "gy", "gz"), None),
        P(("gx", "gy", "gz"), None, None),
        P(("gx", "gy", "gz"), None),
        P(("gx", "gy", "gz")),
        P(("gx", "gy", "gz"), None, None),
        P(("gx", "gy", "gz"), None),
    )
    out_specs = (
        P(("gx", "gy", "gz"), None, None),
        P(("gx", "gy", "gz"), None, None),
        P(("gx", "gy", "gz"), None),
    )
    return jax.shard_map(
        per_device, mesh=mesh, in_specs=in_specs, out_specs=out_specs, check_vma=False
    )
```

profile of v0, /device:TPU:1, one launch (start us, length us, event | category | flops | bytes accessed | tf_op | source)
XLA Modules:
  0.0 1263.7 jit_solution(9198313418127251235)
XLA Ops:
  58.9 187.7 %while.53 = (s32[]{:T(128)}, f32[128,128]{1,0:T(8,128)S(1)}, s32[128,16]{1,0:T(8,128)S(1)}, f32[236,128]{1,0:T(8,128)S(1)}, f32[128,3,128]{2,1,0:T(4,128)S(1)}, ...) while((s32[]{:T(128)}, f32[128,128]{1,0:T(8,128)S(1)}, ...), condition=%wide.region_5.6_spmd, body=%wide.region_2.5_spmd.sunk | while | flops 125831688 | bytes 71256216 | solution.py:71
  61.3 28.7 %multiply_reduce_fusion.4 = f32[128,128,512]{2,1,0:T(8,128)} fusion(f32[128,3,512]{2,1,0:T(4,128)S(1)} %bitcast.105, f32[128,3,128]{2,1,0:T(4,128)S(1)} %get-tuple-element.882), kind=kLoop, calls=%fused_computation.19.clone.1 | loop fusion | flops 67108864 | bytes 34537472 | tf_op jit(solution)/shard_map/while/body/eval_jaxpr/reduce_sum | solution.py:30
  108.2 28.7 %multiply_reduce_fusion.4 = f32[128,128,512]{2,1,0:T(8,128)} fusion(f32[128,3,512]{2,1,0:T(4,128)S(1)} %bitcast.105, f32[128,3,128]{2,1,0:T(4,128)S(1)} %get-tuple-element.882), kind=kLoop, calls=%fused_computation.19.clone.1 | loop fusion | flops 67108864 | bytes 34537472 | tf_op jit(solution)/shard_map/while/body/eval_jaxpr/reduce_sum | solution.py:30
  155.1 28.7 %multiply_reduce_fusion.4 = f32[128,128,512]{2,1,0:T(8,128)} fusion(f32[128,3,512]{2,1,0:T(4,128)S(1)} %bitcast.105, f32[128,3,128]{2,1,0:T(4,128)S(1)} %get-tuple-element.882), kind=kLoop, calls=%fused_computation.19.clone.1 | loop fusion | flops 67108864 | bytes 34537472 | tf_op jit(solution)/shard_map/while/body/eval_jaxpr/reduce_sum | solution.py:30
  202.0 28.7 %multiply_reduce_fusion.4 = f32[128,128,512]{2,1,0:T(8,128)} fusion(f32[128,3,512]{2,1,0:T(4,128)S(1)} %bitcast.105, f32[128,3,128]{2,1,0:T(4,128)S(1)} %get-tuple-element.882), kind=kLoop, calls=%fused_computation.19.clone.1 | loop fusion | flops 67108864 | bytes 34537472 | tf_op jit(solution)/shard_map/while/body/eval_jaxpr/reduce_sum | solution.py:30
  295.0 329.4 %while.54 = (s32[]{:T(128)}, f32[128,3,128]{2,1,0:T(4,128)S(1)}, s32[128,16]{1,0:T(8,128)S(1)}, f32[236,128]{1,0:T(8,128)S(1)}, f32[128,128]{1,0:T(8,128)S(1)}, ...) while((s32[]{:T(128)}, f32[128,3,128]{2,1,0:T(4,128)S(1)}, ...), condition=%wide.region_10.11_spmd, body=%wide.region_7.10_spmd.sunk | while | flops 201378304 | bytes 141250736 | solution.py:87
  297.3 28.8 %fusion.80 = f32[128,128,512]{2,1,0:T(8,128)} fusion(f32[128,3,512]{2,1,0:T(4,128)S(1)} %bitcast.101, f32[128,3,128]{2,1,0:T(4,128)S(1)} %get-tuple-element.918), kind=kLoop, calls=%fused_computation.27.clone.1 | loop fusion | flops 67108864 | bytes 34537472 | tf_op jit(solution)/shard_map/while/body/eval_jaxpr/reduce_sum | solution.py:37
  328.3 24.9 %multiply_multiply_fusion.10 = f32[128,128,512]{2,1,0:T(8,128)} fusion(f32[128,128,512]{2,1,0:T(8,128)} %fusion.80, f32[128,512]{1,0:T(8,128)S(1)} %add.862, f32[128,128]{1,0:T(8,128)S(1)} %get-tuple-element.916, f32[128,512]{1,0:T(8,128)S(1)} %mul.747), kind=kLoop, calls=%fused_computation.29.clone.1 | loop fusion | flops 58720256 | bytes 67698688 | tf_op jit(solution)/shard_map/while/body/eval_jaxpr/mul | solution.py:40
  353.2 23.7 %fusion.81 = f32[128,3,128]{2,1,0:T(4,128)S(1)} fusion(f32[128,128,512]{2,1,0:T(8,128)} %multiply_multiply_fusion.10, f32[128,3,512]{2,1,0:T(4,128)S(1)} %bitcast.102, f32[128,3,128]{2,1,0:T(4,128)S(1)} %get-tuple-element.918), kind=kLoop, calls=%fused_computation.28.clone.1 | loop fusion | flops 75448320 | bytes 34734080 | tf_op jit(solution)/shard_map/while/body/eval_jaxpr/reduce_sum | solution.py:42
  379.6 28.8 %fusion.80 = f32[128,128,512]{2,1,0:T(8,128)} fusion(f32[128,3,512]{2,1,0:T(4,128)S(1)} %bitcast.101, f32[128,3,128]{2,1,0:T(4,128)S(1)} %get-tuple-element.918), kind=kLoop, calls=%fused_computation.27.clone.1 | loop fusion | flops 67108864 | bytes 34537472 | tf_op jit(solution)/shard_map/while/body/eval_jaxpr/reduce_sum | solution.py:37
  410.6 24.9 %multiply_multiply_fusion.10 = f32[128,128,512]{2,1,0:T(8,128)} fusion(f32[128,128,512]{2,1,0:T(8,128)} %fusion.80, f32[128,512]{1,0:T(8,128)S(1)} %add.862, f32[128,128]{1,0:T(8,128)S(1)} %get-tuple-element.916, f32[128,512]{1,0:T(8,128)S(1)} %mul.747), kind=kLoop, calls=%fused_computation.29.clone.1 | loop fusion | flops 58720256 | bytes 67698688 | tf_op jit(solution)/shard_map/while/body/eval_jaxpr/mul | solution.py:40
  435.6 23.7 %fusion.81 = f32[128,3,128]{2,1,0:T(4,128)S(1)} fusion(f32[128,128,512]{2,1,0:T(8,128)} %multiply_multiply_fusion.10, f32[128,3,512]{2,1,0:T(4,128)S(1)} %bitcast.102, f32[128,3,128]{2,1,0:T(4,128)S(1)} %get-tuple-element.918), kind=kLoop, calls=%fused_computation.28.clone.1 | loop fusion | flops 75448320 | bytes 34734080 | tf_op jit(solution)/shard_map/while/body/eval_jaxpr/reduce_sum | solution.py:42
  462.0 28.8 %fusion.80 = f32[128,128,512]{2,1,0:T(8,128)} fusion(f32[128,3,512]{2,1,0:T(4,128)S(1)} %bitcast.101, f32[128,3,128]{2,1,0:T(4,128)S(1)} %get-tuple-element.918), kind=kLoop, calls=%fused_computation.27.clone.1 | loop fusion | flops 67108864 | bytes 34537472 | tf_op jit(solution)/shard_map/while/body/eval_jaxpr/reduce_sum | solution.py:37
  493.0 24.9 %multiply_multiply_fusion.10 = f32[128,128,512]{2,1,0:T(8,128)} fusion(f32[128,128,512]{2,1,0:T(8,128)} %fusion.80, f32[128,512]{1,0:T(8,128)S(1)} %add.862, f32[128,128]{1,0:T(8,128)S(1)} %get-tuple-element.916, f32[128,512]{1,0:T(8,128)S(1)} %mul.747), kind=kLoop, calls=%fused_computation.29.clone.1 | loop fusion | flops 58720256 | bytes 67698688 | tf_op jit(solution)/shard_map/while/body/eval_jaxpr/mul | solution.py:40
  517.9 23.7 %fusion.81 = f32[128,3,128]{2,1,0:T(4,128)S(1)} fusion(f32[128,128,512]{2,1,0:T(8,128)} %multiply_multiply_fusion.10, f32[128,3,512]{2,1,0:T(4,128)S(1)} %bitcast.102, f32[128,3,128]{2,1,0:T(4,128)S(1)} %get-tuple-element.918), kind=kLoop, calls=%fused_computation.28.clone.1 | loop fusion | flops 75448320 | bytes 34734080 | tf_op jit(solution)/shard_map/while/body/eval_jaxpr/reduce_sum | solution.py:42
  544.3 28.8 %fusion.80 = f32[128,128,512]{2,1,0:T(8,128)} fusion(f32[128,3,512]{2,1,0:T(4,128)S(1)} %bitcast.101, f32[128,3,128]{2,1,0:T(4,128)S(1)} %get-tuple-element.918), kind=kLoop, calls=%fused_computation.27.clone.1 | loop fusion | flops 67108864 | bytes 34537472 | tf_op jit(solution)/shard_map/while/body/eval_jaxpr/reduce_sum | solution.py:37
  575.3 24.9 %multiply_multiply_fusion.10 = f32[128,128,512]{2,1,0:T(8,128)} fusion(f32[128,128,512]{2,1,0:T(8,128)} %fusion.80, f32[128,512]{1,0:T(8,128)S(1)} %add.862, f32[128,128]{1,0:T(8,128)S(1)} %get-tuple-element.916, f32[128,512]{1,0:T(8,128)S(1)} %mul.747), kind=kLoop, calls=%fused_computation.29.clone.1 | loop fusion | flops 58720256 | bytes 67698688 | tf_op jit(solution)/shard_map/while/body/eval_jaxpr/mul | solution.py:40
  600.3 23.7 %fusion.81 = f32[128,3,128]{2,1,0:T(4,128)S(1)} fusion(f32[128,128,512]{2,1,0:T(8,128)} %multiply_multiply_fusion.10, f32[128,3,512]{2,1,0:T(4,128)S(1)} %bitcast.102, f32[128,3,128]{2,1,0:T(4,128)S(1)} %get-tuple-element.918), kind=kLoop, calls=%fused_computation.28.clone.1 | loop fusion | flops 75448320 | bytes 34734080 | tf_op jit(solution)/shard_map/while/body/eval_jaxpr/reduce_sum | solution.py:42
  694.3 187.7 %while.55 = (s32[]{:T(128)}, f32[128,128]{1,0:T(8,128)S(1)}, s32[128,16]{1,0:T(8,128)S(1)}, f32[236,128]{1,0:T(8,128)S(1)}, f32[128,3,128]{2,1,0:T(4,128)S(1)}, ...) while((s32[]{:T(128)}, f32[128,128]{1,0:T(8,128)S(1)}, ...), condition=%wide.region_21.22_spmd, body=%wide.region_18.21_spmd.sunk | while | flops 125831688 | bytes 71256216 | solution.py:71
  696.6 28.7 %multiply_reduce_fusion.5 = f32[128,128,512]{2,1,0:T(8,128)} fusion(f32[128,3,512]{2,1,0:T(4,128)S(1)} %bitcast.106, f32[128,3,128]{2,1,0:T(4,128)S(1)} %get-tuple-element.948), kind=kLoop, calls=%fused_computation.33.clone.1 | loop fusion | flops 67108864 | bytes 34537472 | tf_op jit(solution)/shard_map/while/body/eval_jaxpr/reduce_sum | solution.py:30
  743.5 28.7 %multiply_reduce_fusion.5 = f32[128,128,512]{2,1,0:T(8,128)} fusion(f32[128,3,512]{2,1,0:T(4,128)S(1)} %bitcast.106, f32[128,3,128]{2,1,0:T(4,128)S(1)} %get-tuple-element.948), kind=kLoop, calls=%fused_computation.33.clone.1 | loop fusion | flops 67108864 | bytes 34537472 | tf_op jit(solution)/shard_map/while/body/eval_jaxpr/reduce_sum | solution.py:30
  790.4 28.7 %multiply_reduce_fusion.5 = f32[128,128,512]{2,1,0:T(8,128)} fusion(f32[128,3,512]{2,1,0:T(4,128)S(1)} %bitcast.106, f32[128,3,128]{2,1,0:T(4,128)S(1)} %get-tuple-element.948), kind=kLoop, calls=%fused_computation.33.clone.1 | loop fusion | flops 67108864 | bytes 34537472 | tf_op jit(solution)/shard_map/while/body/eval_jaxpr/reduce_sum | solution.py:30
  837.4 28.7 %multiply_reduce_fusion.5 = f32[128,128,512]{2,1,0:T(8,128)} fusion(f32[128,3,512]{2,1,0:T(4,128)S(1)} %bitcast.106, f32[128,3,128]{2,1,0:T(4,128)S(1)} %get-tuple-element.948), kind=kLoop, calls=%fused_computation.33.clone.1 | loop fusion | flops 67108864 | bytes 34537472 | tf_op jit(solution)/shard_map/while/body/eval_jaxpr/reduce_sum | solution.py:30
  931.1 329.4 %while.56 = (s32[]{:T(128)}, f32[128,3,128]{2,1,0:T(4,128)S(1)}, s32[128,16]{1,0:T(8,128)S(1)}, f32[236,128]{1,0:T(8,128)S(1)}, f32[128,128]{1,0:T(8,128)S(1)}, ...) while((s32[]{:T(128)}, f32[128,3,128]{2,1,0:T(4,128)S(1)}, ...), condition=%wide.region_26.27_spmd, body=%wide.region_23.26_spmd.sunk | while | flops 201378304 | bytes 141250736 | solution.py:87
  933.4 28.8 %fusion.83 = f32[128,128,512]{2,1,0:T(8,128)} fusion(f32[128,3,512]{2,1,0:T(4,128)S(1)} %bitcast.103, f32[128,3,128]{2,1,0:T(4,128)S(1)} %get-tuple-element.984), kind=kLoop, calls=%fused_computation.41.clone.1 | loop fusion | flops 67108864 | bytes 34537472 | tf_op jit(solution)/shard_map/while/body/eval_jaxpr/reduce_sum | solution.py:37
  964.4 24.9 %multiply_multiply_fusion.11 = f32[128,128,512]{2,1,0:T(8,128)} fusion(f32[128,128,512]{2,1,0:T(8,128)} %fusion.83, f32[128,512]{1,0:T(8,128)S(1)} %add.874, f32[128,128]{1,0:T(8,128)S(1)} %get-tuple-element.982, f32[128,512]{1,0:T(8,128)S(1)} %mul.764), kind=kLoop, calls=%fused_computation.43.clone.1 | loop fusion | flops 58720256 | bytes 67698688 | tf_op jit(solution)/shard_map/while/body/eval_jaxpr/mul | solution.py:40
  1015.7 28.8 %fusion.83 = f32[128,128,512]{2,1,0:T(8,128)} fusion(f32[128,3,512]{2,1,0:T(4,128)S(1)} %bitcast.103, f32[128,3,128]{2,1,0:T(4,128)S(1)} %get-tuple-element.984), kind=kLoop, calls=%fused_computation.41.clone.1 | loop fusion | flops 67108864 | bytes 34537472 | tf_op jit(solution)/shard_map/while/body/eval_jaxpr/reduce_sum | solution.py:37
  1046.8 24.9 %multiply_multiply_fusion.11 = f32[128,128,512]{2,1,0:T(8,128)} fusion(f32[128,128,512]{2,1,0:T(8,128)} %fusion.83, f32[128,512]{1,0:T(8,128)S(1)} %add.874, f32[128,128]{1,0:T(8,128)S(1)} %get-tuple-element.982, f32[128,512]{1,0:T(8,128)S(1)} %mul.764), kind=kLoop, calls=%fused_computation.43.clone.1 | loop fusion | flops 58720256 | bytes 67698688 | tf_op jit(solution)/shard_map/while/body/eval_jaxpr/mul | solution.py:40
  1098.1 28.8 %fusion.83 = f32[128,128,512]{2,1,0:T(8,128)} fusion(f32[128,3,512]{2,1,0:T(4,128)S(1)} %bitcast.103, f32[128,3,128]{2,1,0:T(4,128)S(1)} %get-tuple-element.984), kind=kLoop, calls=%fused_computation.41.clone.1 | loop fusion | flops 67108864 | bytes 34537472 | tf_op jit(solution)/shard_map/while/body/eval_jaxpr/reduce_sum | solution.py:37
  1129.1 24.9 %multiply_multiply_fusion.11 = f32[128,128,512]{2,1,0:T(8,128)} fusion(f32[128,128,512]{2,1,0:T(8,128)} %fusion.83, f32[128,512]{1,0:T(8,128)S(1)} %add.874, f32[128,128]{1,0:T(8,128)S(1)} %get-tuple-element.982, f32[128,512]{1,0:T(8,128)S(1)} %mul.764), kind=kLoop, calls=%fused_computation.43.clone.1 | loop fusion | flops 58720256 | bytes 67698688 | tf_op jit(solution)/shard_map/while/body/eval_jaxpr/mul | solution.py:40
  1180.4 28.8 %fusion.83 = f32[128,128,512]{2,1,0:T(8,128)} fusion(f32[128,3,512]{2,1,0:T(4,128)S(1)} %bitcast.103, f32[128,3,128]{2,1,0:T(4,128)S(1)} %get-tuple-element.984), kind=kLoop, calls=%fused_computation.41.clone.1 | loop fusion | flops 67108864 | bytes 34537472 | tf_op jit(solution)/shard_map/while/body/eval_jaxpr/reduce_sum | solution.py:37
  1211.5 24.9 %multiply_multiply_fusion.11 = f32[128,128,512]{2,1,0:T(8,128)} fusion(f32[128,128,512]{2,1,0:T(8,128)} %fusion.83, f32[128,512]{1,0:T(8,128)S(1)} %add.874, f32[128,128]{1,0:T(8,128)S(1)} %get-tuple-element.982, f32[128,512]{1,0:T(8,128)S(1)} %mul.764), kind=kLoop, calls=%fused_computation.43.clone.1 | loop fusion | flops 58720256 | bytes 67698688 | tf_op jit(solution)/shard_map/while/body/eval_jaxpr/mul | solution.py:40
  (336 shorter events, 505.8 us)
Async XLA Ops:
  9.6 25.1 %collective-permute-start = (f32[1,3,3,4,4,128]{5,4,3,2,1,0:T(4,128)S(1)}, f32[1,3,3,4,4,128]{5,4,3,2,1,0:T(4,128)S(1)}, u32[]{:S(2)}, u32[]{:S(2)}) collective-permute-start(f32[1,3,3,4,4,128]{5,4,3,2,1,0:T(4,128)S(1)} %bitcast.126), channel_id=1, source_target_pairs={{0,32},{32,64},{64,96},{1,33},{33,65},{65,97},{2,34},{34,66},{66,9... | collective-permute-start | bytes 221192 | tf_op jit(solution)/shard_map/ppermute | solution.py:20
  13.6 21.1 %collective-permute-start.1 = (f32[1,3,3,4,4,128]{5,4,3,2,1,0:T(4,128)S(1)}, f32[1,3,3,4,4,128]{5,4,3,2,1,0:T(4,128)S(1)}, u32[]{:S(2)}, u32[]{:S(2)}) collective-permute-start(f32[1,3,3,4,4,128]{5,4,3,2,1,0:T(4,128)S(1)} %bitcast.125), channel_id=1, source_target_pairs={{32,0},{64,32},{96,64},{33,1},{65,33},{97,65},{34,2},{66,34},{98,6... | collective-permute-start | bytes 221192 | tf_op jit(solution)/shard_map/ppermute | solution.py:23
  34.8 5.4 collective-permute-start.2
  38.4 5.8 collective-permute-start.3
  44.3 7.9 collective-permute-start.4
  49.5 7.1 collective-permute-start.5
  247.4 5.7 collective-permute-start.6
  251.7 4.5 collective-permute-start.7
  256.2 5.0 collective-permute-start.8
  259.8 4.6 collective-permute-start.9
  264.4 8.8 collective-permute-start.10
  269.1 5.4 collective-permute-start.11
  294.9 330.7 %copy-start.4 = (f32[128,128]{1,0:T(8,128)S(1)}, f32[128,128]{1,0:T(8,128)}, u32[]{:S(2)}) copy-start(f32[128,128]{1,0:T(8,128)} %param.32) | copy-start | bytes 196612
  294.9 359.0 %copy-start.6 = (s32[1024]{0:T(1024)S(1)}, s32[1024]{0:T(1024)}, u32[]{:S(2)}) copy-start(s32[1024]{0:T(1024)} %get-tuple-element.684) | copy-start | bytes 12292
  630.7 16.7 %collective-permute-start.12 = (f32[1,2,8,128]{3,2,1,0:T(8,128)S(1)}, f32[1,2,8,128]{3,2,1,0:T(8,128)S(1)}, u32[]{:S(2)}, u32[]{:S(2)}) collective-permute-start(f32[1,2,8,128]{3,2,1,0:T(8,128)S(1)} %get-tuple-element.675), channel_id=1, source_target_pairs={{0,32},{32,64},{64,96},{1,33},{33,65},{65,97},{2,34},{34,66},{66,9... | collective-permute-start | bytes 24584 | tf_op jit(solution)/shard_map/ppermute | solution.py:20
  634.1 15.2 %collective-permute-start.13 = (f32[1,2,8,128]{3,2,1,0:T(8,128)S(1)}, f32[1,2,8,128]{3,2,1,0:T(8,128)S(1)}, u32[]{:S(2)}, u32[]{:S(2)}) collective-permute-start(f32[1,2,8,128]{3,2,1,0:T(8,128)S(1)} %get-tuple-element.674), channel_id=1, source_target_pairs={{32,0},{64,32},{96,64},{33,1},{65,33},{97,65},{34,2},{66,34},{98,6... | collective-permute-start | bytes 24584 | tf_op jit(solution)/shard_map/ppermute | solution.py:23
  635.4 14.0 %collective-permute-start.14 = (f32[1,2,8,128]{3,2,1,0:T(8,128)S(1)}, f32[1,2,8,128]{3,2,1,0:T(8,128)S(1)}, u32[]{:S(2)}, u32[]{:S(2)}) collective-permute-start(f32[1,2,8,128]{3,2,1,0:T(8,128)S(1)} %get-tuple-element.673), channel_id=1, source_target_pairs={{0,8},{8,16},{16,24},{1,9},{9,17},{17,25},{2,10},{10,18},{18,26},{... | collective-permute-start | bytes 24584 | tf_op jit(solution)/shard_map/ppermute | solution.py:20
  638.7 10.7 collective-permute-start.15
  640.0 9.5 collective-permute-start.16
  647.4 5.0 collective-permute-start.17
  655.6 6.5 collective-permute-start.18
  659.8 5.1 collective-permute-start.19
  665.0 17.2 %collective-permute-start.20 = (f32[5,1,3,4,4,128]{5,4,3,2,1,0:T(4,128)S(1)}, f32[5,1,3,4,4,128]{5,4,3,2,1,0:T(4,128)S(1)}, u32[]{:S(2)}, u32[]{:S(2)}) collective-permute-start(f32[5,1,3,4,4,128]{5,4,3,2,1,0:T(4,128)S(1)} %get-tuple-element.650), channel_id=1, source_target_pairs={{0,8},{8,16},{16,24},{1,9},{9,17},{17,25},{2,10},{10,18},{18,26},{... | collective-permute-start | bytes 368648 | tf_op jit(solution)/shard_map/ppermute | solution.py:20
  669.3 13.0 %collective-permute-start.21 = (f32[5,1,3,4,4,128]{5,4,3,2,1,0:T(4,128)S(1)}, f32[5,1,3,4,4,128]{5,4,3,2,1,0:T(4,128)S(1)}, u32[]{:S(2)}, u32[]{:S(2)}) collective-permute-start(f32[5,1,3,4,4,128]{5,4,3,2,1,0:T(4,128)S(1)} %get-tuple-element.651), channel_id=1, source_target_pairs={{8,0},{16,8},{24,16},{9,1},{17,9},{25,17},{10,2},{18,10},{26,18},{... | collective-permute-start | bytes 368648 | tf_op jit(solution)/shard_map/ppermute | solution.py:23
  682.4 10.7 collective-permute-start.22
  686.5 7.1 collective-permute-start.23
  882.8 4.3 collective-permute-start.24
  885.7 4.5 collective-permute-start.25
  890.2 5.6 collective-permute-start.26
  894.5 4.6 collective-permute-start.27
  899.2 8.2 collective-permute-start.28
  905.2 5.4 collective-permute-start.29
  (8 other events, 1410.8 us)
where the time goes:
time: 1270 us; the launch traced here: 1260 us
  other arithmetic  1060 us (83%)
  starting transfers between devices  83.7 us (7%)
  local copies, waits for them, and re-layouts  81.8 us (6%)
  waiting for transfers between devices  32.4 us (3%)
    reduce_sum x10, other arithmetic, pair_density(): squared = jnp.sum(offset * offset, axis=1)  252 us
    reduce_sum x8, other arithmetic, pair_force(): squared = jnp.sum(offset * offset, axis=1)  231 us
    reduce_sum x10, other arithmetic, pair_force(): jnp.sum(weight[:, None, :, :] * offset, axis=3)  219 us
    mul x10, other arithmetic, pair_force(): away_mass[:, None, :] * (home_term[:, :, None] + away_term[:, None, :])  210 us
    reduce_sum x10, other arithmetic, pair_density(): return jnp.sum(away_mass[:, None, :] * (kernel * kernel * kernel), axis=2)  128 us
    ppermute x15, starting transfers between devices, padded_2(): lax.ppermute(lax.slice_in_dim(block, block.shape[dim] - width, None, axis...  60.5 us
    gather x16, local copies, waits for them, and re-layouts, joined_points(): chosen = all_points[picked]  33.2 us
    ppermute x15, waiting for transfers between devices, padded_2(): lax.ppermute(lax.slice_in_dim(block, 0, width, axis=dim), axis, backward)  31.8 us
  transfers between devices with their start and end apart: 30, of which 12 were waited for; matrix products, arithmetic and copies ran while one was open for 4% of the time, Pallas kernels for 0%

commit v1 on v0

v1 whole, which is shorter than its diff:
```python
import jax
import jax.numpy as jnp
from jax import lax
from jax.experimental import pallas as pl
from jax.experimental.pallas import tpu as pltpu
from jax.sharding import PartitionSpec as P

AXES = ("gx", "gy", "gz")
BLOCKS = 128
WIDTH = 128
GHOST_CAP = 4
MOVE_CAP = 2
NEIGHBOURS = 16
CODES = 27
STORED = BLOCKS + CODES * GHOST_CAP
TERMS = 48
time_step = 0.25
VMEM_LIMIT = 60 << 20

f32 = jnp.float32
bf16 = jnp.bfloat16
VMEM = pl.BlockSpec(memory_space=pltpu.VMEM)
SMEM = pl.BlockSpec(memory_space=pltpu.SMEM)


def shape(*dims, dtype=f32):
    return jax.ShapeDtypeStruct(dims, dtype)


def call(kernel, name, in_specs, out_shape, scratch=()):
    many = isinstance(out_shape, (list, tuple))
    return pl.pallas_call(
        kernel,
        in_specs=in_specs,
        out_specs=[VMEM] * len(out_shape) if many else VMEM,
        out_shape=out_shape,
        scratch_shapes=list(scratch),
        compiler_params=pltpu.CompilerParams(vmem_limit_bytes=VMEM_LIMIT),
        name=name,
    )


def near_device(place, code):
    ix = jnp.clip(place[1] + code // 9 - 1, 0, place[4] - 1)
    iy = jnp.clip(place[2] + code // 3 % 3 - 1, 0, place[5] - 1)
    iz = jnp.clip(place[3] + code % 3 - 1, 0, place[6] - 1)
    return (ix * place[5] + iy) * place[6] + iz


def fill_sends(place, send, out, load):
    def one(code, carry):
        device = near_device(place, code)
        for slot in range(GHOST_CAP):
            row = jnp.maximum(send[device, slot], 0)
            out[device, slot] = load(row)
        return carry

    lax.fori_loop(0, CODES, one, 0)


def parts_of(value):
    high = value.astype(bf16).astype(f32)
    rest = value - high
    middle = rest.astype(bf16).astype(f32)
    return high, middle, rest - middle


def away_terms(rows):
    high, middle, low = parts_of(rows)
    return jnp.concatenate([high, middle, high, middle, low, high], axis=0).astype(bf16)


def home_terms(rows):
    high, middle, low = parts_of(rows)
    return jnp.concatenate([high, high, middle, middle, high, low], axis=0)


def prepare(place, stored, points, mass, away_density, away_force, local):
    axis = [points[k : k + 1] - (place[1 + k].astype(f32) + 0.5) for k in range(3)]
    square = axis[0] * axis[0] + axis[1] * axis[1] + axis[2] * axis[2]
    one = jnp.ones_like(square)
    nil = jnp.zeros_like(square)
    away = jnp.concatenate(
        [1.0 - 4.0 * square] + [8.0 * a for a in axis] + [-4.0 * one, nil, nil, nil], axis=0
    )
    away_density[stored] = away_terms(jnp.exp(jnp.log(mass) * (1.0 / 3.0)) * away)
    away_force[stored] = away_terms(jnp.sqrt(mass) * away)
    home = jnp.concatenate([one] + axis + [square, nil, nil, nil], axis=0)
    local[stored] = jnp.concatenate(axis + [one, one, one, one, one], axis=0)
    return home


def lane_sums(values):
    return jnp.sum(values.T, axis=0, keepdims=True)


def density_kernel(place, lookup, send, points, mass, ghosts, rho, rho_send, away_force, home, local, away_density):
    def own(block, carry):
        rows = prepare(place, block, points[block], mass[pl.ds(block, 1)], away_density, away_force, local)
        home[block] = home_terms(rows).T.astype(bf16)
        return carry

    lax.fori_loop(0, BLOCKS, own, 0)

    def other(code, carry):
        device = near_device(place, code)
        for slot in range(GHOST_CAP):
            block = ghosts[device, slot]
            prepare(place, BLOCKS + code * GHOST_CAP + slot, block[0:3], block[3:4], away_density, away_force, local)
        return carry

    lax.fori_loop(0, CODES, other, 0)

    unroll = 4

    def some(step, carry):
        for part in range(unroll):
            block = step * unroll + part
            left = home[block]
            names = [block] + [lookup[block, n] for n in range(NEIGHBOURS)]
            total = jnp.zeros((WIDTH, WIDTH), f32)
            for first in range(0, NEIGHBOURS + 1, 2):
                some_names = names[first : first + 2]
                right = jnp.concatenate([away_density[n] for n in some_names], axis=1)
                kernel = jnp.maximum(jnp.dot(left, right, preferred_element_type=f32), 0.0)
                cube = kernel * kernel * kernel
                for k in range(len(some_names)):
                    total = total + cube[:, k * WIDTH : (k + 1) * WIDTH]
            rho[pl.ds(block, 1)] = lane_sums(total)
        return carry

    lax.fori_loop(0, BLOCKS // unroll, some, 0)

    def one(code, carry):
        device = near_device(place, code)
        for slot in range(GHOST_CAP):
            row = jnp.maximum(send[device, slot], 0)
            rho_send[device, pl.ds(slot, 1)] = rho[pl.ds(row, 1)]
        return carry

    lax.fori_loop(0, CODES, one, 0)


def pressure(density):
    return jnp.exp(jnp.log(density) * (-1.0 / 3.0))


def force_kernel(place, lookup, rho, rho_ghosts, away_force, home, local, emit):
    def own(block, carry):
        local[block, 3:4] = pressure(rho[pl.ds(block, 1)])
        return carry

    lax.fori_loop(0, BLOCKS, own, 0)

    def other(code, carry):
        device = near_device(place, code)
        values = pressure(rho_ghosts[device])
        for slot in range(GHOST_CAP):
            local[BLOCKS + code * GHOST_CAP + slot, 3:4] = values[slot : slot + 1]
        return carry

    lax.fori_loop(0, CODES, other, 0)

    unroll = 2

    def some(step, carry):
        for part in range(unroll):
            block = step * unroll + part
            left = home[block]
            mine = local[block]
            names = [block] + [lookup[block, n] for n in range(NEIGHBOURS)]
            own_term = jnp.broadcast_to(mine[3:4], (WIDTH, WIDTH)).T
            total = [jnp.zeros((WIDTH, WIDTH), f32) for _ in range(4)]
            for first in range(0, NEIGHBOURS + 1, 2):
                some_names = names[first : first + 2]
                right = jnp.concatenate([away_force[n] for n in some_names], axis=1)
                kernel = jnp.maximum(jnp.dot(left, right, preferred_element_type=f32), 0.0)
                for k, name in enumerate(some_names):
                    this = kernel[:, k * WIDTH : (k + 1) * WIDTH]
                    weight = this * this * (own_term + local[name, 3:4])
                    total[3] = total[3] + weight
                    for c in range(3):
                        total[c] = total[c] + weight * local[name, c : c + 1]
            whole = lane_sums(total[3])
            pull = [24.0 * (mine[c : c + 1] * whole - lane_sums(total[c])) for c in range(3)]
            emit(block, jnp.concatenate(pull, axis=0))
        return carry

    lax.fori_loop(0, BLOCKS // unroll, some, 0)


def move_kernel(place, target, state, stay, outbox):
    outbox[...] = jnp.zeros_like(outbox)

    def one(block, counts):
        goal = target[block]
        device = goal // BLOCKS
        spot = goal % BLOCKS
        rows = state[block]
        here = device == place[0]

        @pl.when(here)
        def _():
            stay[spot] = rows

        dx = device // (place[5] * place[6]) - place[1]
        dy = device // place[6] % place[5] - place[2]
        dz = device % place[6] - place[3]
        heading = jnp.where(
            dx != 0,
            jnp.where(dx > 0, 1, 0),
            jnp.where(dy != 0, jnp.where(dy > 0, 3, 2), jnp.where(dz > 0, 5, 4)),
        )
        used = counts[0]
        for k in range(1, 6):
            used = jnp.where(heading == k, counts[k], used)

        @pl.when(jnp.logical_not(here))
        def _():
            slot = heading * MOVE_CAP + jnp.minimum(used, MOVE_CAP - 1)
            outbox[slot, 0:7] = rows[0:7]
            outbox[slot, 7:8] = jnp.full((1, WIDTH), spot + 1, jnp.int32).astype(f32)

        gone = jnp.where(here, 0, 1)
        return tuple(counts[k] + jnp.where(heading == k, gone, 0) for k in range(6))

    lax.fori_loop(0, BLOCKS, one, (jnp.int32(0),) * 6)


def merge_kernel(place, labels, send, stay, arrived, points, velocity, mass, ghost_send):
    def put(spot, rows):
        points[spot] = rows[0:3]
        velocity[spot] = rows[3:6]
        mass[pl.ds(spot, 1)] = rows[6:7]

    def copy(block, carry):
        put(block, stay[block])
        return carry

    lax.fori_loop(0, BLOCKS, copy, 0)
    for k in range(6 * MOVE_CAP):

        @pl.when(labels[k] > 0)
        def _():
            put(labels[k] - 1, arrived[k])

    def load(row):
        return jnp.concatenate([points[row], mass[pl.ds(row, 1)]], axis=0)

    fill_sends(place, send, ghost_send, load)


def pack_kernel(place, send, points, mass, ghost_send):
    def load(row):
        return jnp.concatenate([points[row], mass[pl.ds(row, 1)]], axis=0)

    fill_sends(place, send, ghost_send, load)


def last_force_kernel(place, lookup, rho, rho_ghosts, away_force, home, local_in, points, velocity, points_out, velocity_out, local):
    local[...] = local_in[...]

    def emit(block, pull):
        speed = velocity[block] + time_step * pull
        velocity_out[block] = speed
        points_out[block] = points[block] + time_step * speed

    force_kernel(place, lookup, rho, rho_ghosts, away_force, home, local, emit)


def table_rows(neighbours):
    size_y = lax.axis_size("gy")
    size_z = lax.axis_size("gz")
    remote = jnp.maximum(neighbours - BLOCKS, 0)
    source = remote // GHOST_CAP
    within = remote % GHOST_CAP
    code = (source // (size_y * size_z) - lax.axis_index("gx") + 1) * 9
    code = code + (source // size_z % size_y - lax.axis_index("gy") + 1) * 3
    code = code + (source % size_z - lax.axis_index("gz") + 1)
    return jnp.where(neighbours < BLOCKS, neighbours, BLOCKS + code * GHOST_CAP + within)


def to_all(values):
    return lax.all_to_all(values, AXES, 0, 0, tiled=True)


def shifted(values, axis, step):
    count = lax.axis_size(axis)
    pairs = [(i, i + step) for i in range(count) if 0 <= i + step < count]
    return lax.ppermute(values, axis, pairs)


def densities(place, lookup, send, points, mass, ghost_send, devices):
    ghosts = to_all(ghost_send)
    return call(
        density_kernel,
        "density",
        [SMEM] * 3 + [VMEM] * 3,
        [
            shape(BLOCKS, WIDTH),
            shape(devices, GHOST_CAP, WIDTH),
            shape(STORED, TERMS, WIDTH, dtype=bf16),
            shape(BLOCKS, WIDTH, TERMS, dtype=bf16),
            shape(STORED, 8, WIDTH),
        ],
        [pltpu.VMEM((STORED, TERMS, WIDTH), bf16)],
    )(place, lookup, send, points, mass, ghosts)


def per_device(position, velocity, mass, send_first, neighbours_first, destination, send_second, neighbours_second):
    sizes = [lax.axis_size(a) for a in AXES]
    devices = sizes[0] * sizes[1] * sizes[2]
    place = jnp.stack(
        [lax.axis_index(AXES).astype(jnp.int32)]
        + [lax.axis_index(a).astype(jnp.int32) for a in AXES]
        + [jnp.int32(s) for s in sizes]
    )
    send_first, send_second = send_first[0], send_second[0]
    lookup_first, lookup_second = table_rows(neighbours_first), table_rows(neighbours_second)
    ghost_shape = shape(devices, GHOST_CAP, 4, WIDTH)
    ghost_send = call(pack_kernel, "pack", [SMEM] * 2 + [VMEM] * 2, ghost_shape)(place, send_first, position, mass)
    rho, rho_send, away_force, home, local = densities(
        place, lookup_first, send_first, position, mass, ghost_send, devices
    )
    rho_ghosts = to_all(rho_send)

    def first(place, lookup, rho, rho_ghosts, away_force, home, local_in, points, velocity, mass, state, local):
        local[...] = local_in[...]

        def emit(block, pull):
            speed = velocity[block] + time_step * pull
            state[block, 0:3] = points[block] + time_step * speed
            state[block, 3:6] = speed
            state[block, 6:7] = mass[pl.ds(block, 1)]

        force_kernel(place, lookup, rho, rho_ghosts, away_force, home, local, emit)

    state = call(
        first, "force", [SMEM] * 2 + [VMEM] * 8, shape(BLOCKS, 8, WIDTH), [pltpu.VMEM((STORED, 8, WIDTH), f32)]
    )(place, lookup_first, rho, rho_ghosts, away_force, home, local, position, velocity, mass)
    stay, outbox = call(
        move_kernel,
        "move",
        [SMEM] * 2 + [VMEM],
        [shape(BLOCKS, 8, WIDTH), shape(6 * MOVE_CAP, 8, WIDTH)],
    )(place, destination, state)
    boxes = outbox.reshape(6, MOVE_CAP, 8, WIDTH)
    arrived = jnp.concatenate(
        [shifted(boxes[2 * k + way], axis, 2 * way - 1) for k, axis in enumerate(AXES) for way in (0, 1)], axis=0
    )
    labels = arrived[:, 7, 0].astype(jnp.int32)
    position, velocity, mass, ghost_send = call(
        merge_kernel,
        "merge",
        [SMEM] * 3 + [VMEM] * 2,
        [shape(BLOCKS, 3, WIDTH), shape(BLOCKS, 3, WIDTH), shape(BLOCKS, WIDTH), ghost_shape],
    )(place, labels, send_second, stay, arrived)
    rho, rho_send, away_force, home, local = densities(
        place, lookup_second, send_second, position, mass, ghost_send, devices
    )
    rho_ghosts = to_all(rho_send)
    position, velocity = call(
        last_force_kernel,
        "last_force",
        [SMEM] * 2 + [VMEM] * 7,
        [shape(BLOCKS, 3, WIDTH), shape(BLOCKS, 3, WIDTH)],
        [pltpu.VMEM((STORED, 8, WIDTH), f32)],
    )(place, lookup_second, rho, rho_ghosts, away_force, home, local, position, velocity)
    return position, velocity, rho


def solution(mesh):
    along = P(AXES)
    return jax.shard_map(
        per_device, mesh=mesh, in_specs=(along,) * 8, out_specs=(along,) * 3, check_vma=False
    )
```

time: 1270 us -> 391 us (0.31)
  other arithmetic: 1060 us -> 3.19 us
  Pallas kernels: 0 us -> 272 us
  local copies, waits for them, and re-layouts: 81.8 us -> 13.7 us
  starting transfers between devices: 83.7 us -> 37.9 us
  blocking collectives: 0 us -> 16.3 us
  waiting for transfers between devices: 32.4 us -> 46.1 us
    reduce_sum x39 -> x0, other arithmetic: 830 us -> none  [the longest x10 252 us: pair_density(): squared = jnp.sum(offset * offset, axis=1)]
    pallas_call x0 -> x7, Pallas kernels: none -> 272 us  [the longest x2 101 us: densities(): call(density_kernel, 'density', [SMEM] * 3 + [VMEM] * 3, [shape(BLOCKS, W...]
    mul x12 -> x0, other arithmetic: 210 us -> none  [the longest x10 210 us: pair_force(): away_mass[:, None, :] * (home_term[:, :, None] + away_term[:, None, :])]
    ppermute x30 -> x6, starting transfers between devices: 83.7 us -> 16.5 us  [shifted(): return lax.ppermute(values, axis, pairs)]
    gather x56 -> x0, local copies, waits for them, and re-layouts: 62.5 us -> none  [the longest x16 33.2 us: joined_points(): chosen = all_points[picked]]
    all_to_all x0 -> x3, waiting for transfers between devices: none -> 45.1 us  [to_all(): return lax.all_to_all(values, AXES, 0, 0, tiled=True)]
    ppermute x30 -> x6, waiting for transfers between devices: 32.4 us -> 0.98 us  [shifted(): return lax.ppermute(values, axis, pairs)]
    all_to_all x0 -> x3, starting transfers between devices: none -> 21.4 us  [to_all(): return lax.all_to_all(values, AXES, 0, 0, tiled=True)]
  transfers between devices with their start and end apart: 30 -> 9, of which waited for: 12 -> 4; matrix products, arithmetic and copies ran while one was open for 4% -> 1% of each run, Pallas kernels for 0% -> 0%
where the time goes in v1:
time: 391 us; the launch traced here: 390 us
  Pallas kernels  272 us (70%)
  waiting for transfers between devices  46.1 us (12%)
  starting transfers between devices  37.9 us (10%)
  blocking collectives  16.3 us (4%)
  local copies, waits for them, and re-layouts  13.7 us (4%)
    pallas_call x2, Pallas kernels, densities(): call(density_kernel, 'density', [SMEM] * 3 + [VMEM] * 3, [shape(BLOCKS, W...  101 us
    pallas_call x1, Pallas kernels, per_device(): call(first, 'force', [SMEM] * 2 + [VMEM] * 8, shape(BLOCKS, 8, WIDTH), [p...  76.1 us
    pallas_call x1, Pallas kernels, per_device(): call(last_force_kernel, 'last_force', [SMEM] * 2 + [VMEM] * 7, [shape(BLO...  76 us
    all_to_all x3, waiting for transfers between devices, to_all(): return lax.all_to_all(values, AXES, 0, 0, tiled=True)  45.1 us
    all_to_all x3, starting transfers between devices, to_all(): return lax.all_to_all(values, AXES, 0, 0, tiled=True)  21.4 us
    ppermute x6, starting transfers between devices, shifted(): return lax.ppermute(values, axis, pairs)  16.5 us
    all_to_all x1, blocking collectives, to_all(): return lax.all_to_all(values, AXES, 0, 0, tiled=True)  16.3 us
    unnamed x29, local copies, waits for them, and re-layouts  11.8 us
  transfers between devices with their start and end apart: 9, of which 4 were waited for; matrix products, arithmetic and copies ran while one was open for 1% of the time, Pallas kernels for 0%

profile of v1, /device:TPU:1, one launch (start us, length us, event | category | flops | bytes accessed | tf_op | source)
XLA Modules:
  0.0 390.2 jit_solution(15571712030150865871)
XLA Ops:
  0.7 1.8 copy.58.points
  2.5 1.4 copy.56
  4.6 3.8 pack.1
  8.3 11.5 %all-to-all-start = ((f32[128,4,4,128]{3,2,1,0:T(4,128)}), f32[128,4,4,128]{3,2,1,0:T(4,128)S(1)}, u32[]{:S(2)}, u32[]{:S(2)}) async-start(f32[128,4,4,128]{3,2,1,0:T(4,128)} %pack.1), calls=%async_computation | async-start | bytes 2097152 | tf_op jit(solution)/shard_map/all_to_all | solution.py:284
  19.9 0.8 copy.55
  21.6 0.8 fusion.25.lookup
  22.4 16.8 %all-to-all-done.ghosts = f32[128,4,4,128]{3,2,1,0:T(4,128)S(1)} async-done(((f32[128,4,4,128]{3,2,1,0:T(4,128)}), f32[128,4,4,128]{3,2,1,0:T(4,128)S(1)}, u32[]{:S(2)}, u32[]{:S(2)}) %all-to-all-start) | async-done | bytes 1048608 | tf_op jit(solution)/shard_map/all_to_all | solution.py:284
  39.2 1.0 copy-done.1
  40.2 50.6 %density.2 = (f32[128,128]{1,0:T(8,128)}, f32[128,4,128]{2,1,0:T(4,128)}, bf16[236,48,128]{2,1,0:T(8,128)(2,1)}, bf16[128,128,48]{2,1,0:T(8,128)(2,1)}, f32[236,8,128]{2,1,0:T(8,128)}) custom-call(s32[7]{0:T(128)} %stack.19.place, s32[128,16]{1,0:T(8,128)} %fusion.25.lookup, s32[128,4]{1,0:T(8,128)} %bitcast.9, f32[128,3,128]{2,1,0:T(4,128)} %copy.58.points, ...), custom_call_target="tpu_custom_call" | custom-call | tf_op jit(solution)/shard_map/density/pallas_call | solution.py:295
  90.8 4.3 %all-to-all-start.1 = ((f32[128,4,128]{2,1,0:T(4,128)}), f32[128,4,128]{2,1,0:T(4,128)S(1)}, u32[]{:S(2)}, u32[]{:S(2)}) async-start(f32[128,4,128]{2,1,0:T(4,128)} %get-tuple-element.22), calls=%async_computation.1 | async-start | bytes 524288 | tf_op jit(solution)/shard_map/all_to_all | solution.py:284
  95.1 0.8 copy.60.velocity
  96.0 10.2 %all-to-all-done.1.rho_ghosts = f32[128,4,128]{2,1,0:T(4,128)S(1)} async-done(((f32[128,4,128]{2,1,0:T(4,128)}), f32[128,4,128]{2,1,0:T(4,128)S(1)}, u32[]{:S(2)}, u32[]{:S(2)}) %all-to-all-start.1) | async-done | bytes 262176 | tf_op jit(solution)/shard_map/all_to_all | solution.py:284
  106.9 76.1 %force.1.state = f32[128,8,128]{2,1,0:T(8,128)} custom-call(s32[7]{0:T(128)} %stack.19.place, s32[128,16]{1,0:T(8,128)} %fusion.25.lookup, f32[128,128]{1,0:T(8,128)} %get-tuple-element.21.rho, f32[128,4,128]{2,1,0:T(4,128)} %copy-done.2, bf16[236,48,128]{2,1,0:T(8,128)(2,1)} %get-tuple-element.23.away_force, bf16[128,128,48]{2,1,0:T(8,128)(2,1)} %get-tuple-element.24.home, ...), custom_call_target="tpu_custom_call" | custom-call | tf_op jit(solution)/shard_map/force/pallas_call | solution.py:338
  183.0 10.1 %move.1 = (f32[128,8,128]{2,1,0:T(8,128)}, f32[12,8,128]{2,1,0:T(8,128)}) custom-call(s32[7]{0:T(128)} %stack.19.place, s32[128]{0:T(128)} %target.1, f32[128,8,128]{2,1,0:T(8,128)} %force.1.state), custom_call_target="tpu_custom_call" | custom-call | tf_op jit(solution)/shard_map/move/pallas_call | solution.py:341
  193.9 1.3 collective-permute-start
  195.9 4.0 %collective-permute-start.1 = (f32[2,8,128]{2,1,0:T(8,128)S(1)}, f32[2,8,128]{2,1,0:T(8,128)S(1)}, u32[]{:S(2)}, u32[]{:S(2)}) collective-permute-start(f32[2,8,128]{2,1,0:T(8,128)S(1)} %get-tuple-element.52), channel_id=1, source_target_pairs={{0,32},{32,64},{64,96},{1,33},{33,65},{65,97},{2,34},{34,66},{66,9... | collective-permute-start | bytes 24584 | tf_op jit(solution)/shard_map/ppermute | solution.py:290
  199.9 1.3 collective-permute-start.2
  201.2 4.0 %collective-permute-start.3 = (f32[2,8,128]{2,1,0:T(8,128)S(1)}, f32[2,8,128]{2,1,0:T(8,128)S(1)}, u32[]{:S(2)}, u32[]{:S(2)}) collective-permute-start(f32[2,8,128]{2,1,0:T(8,128)S(1)} %get-tuple-element.50), channel_id=1, source_target_pairs={{0,8},{8,16},{16,24},{1,9},{9,17},{17,25},{2,10},{10,18},{18,26},{... | collective-permute-start | bytes 24584 | tf_op jit(solution)/shard_map/ppermute | solution.py:290
  205.2 4.0 %collective-permute-start.4 = (f32[2,8,128]{2,1,0:T(8,128)S(1)}, f32[2,8,128]{2,1,0:T(8,128)S(1)}, u32[]{:S(2)}, u32[]{:S(2)}) collective-permute-start(f32[2,8,128]{2,1,0:T(8,128)S(1)} %get-tuple-element.49), channel_id=1, source_target_pairs={{1,0},{2,1},{3,2},{4,3},{5,4},{6,5},{7,6},{9,8},{10,9},{11,10},{12... | collective-permute-start | bytes 24584 | tf_op jit(solution)/shard_map/ppermute | solution.py:290
  209.2 2.0 collective-permute-start.5
  211.3 1.0 collective-permute-done.5
  212.3 0.8 fusion.38.labels
  213.1 5.0 %merge.1 = (f32[128,3,128]{2,1,0:T(4,128)}, f32[128,3,128]{2,1,0:T(4,128)}, f32[128,128]{1,0:T(8,128)}, f32[128,4,4,128]{3,2,1,0:T(4,128)}) custom-call(s32[7]{0:T(128)} %stack.19.place, s32[12]{0:T(128)} %fusion.38.labels, s32[128,4]{1,0:T(8,128)} %bitcast.6, f32[128,8,128]{2,1,0:T(8,128)} %get-tuple-element.27.stay, f32[12,8,128]{2,1,0:T(8,128)} %copy-done.4), custom_call_target="tpu_custom_call" | custom-call | tf_op jit(solution)/shard_map/merge/pallas_call | solution.py:352
  218.1 5.6 %all-to-all-start.2 = ((f32[128,4,4,128]{3,2,1,0:T(4,128)}), f32[128,4,4,128]{3,2,1,0:T(4,128)S(1)}, u32[]{:S(2)}, u32[]{:S(2)}) async-start(f32[128,4,4,128]{3,2,1,0:T(4,128)} %get-tuple-element.30), calls=%async_computation.2 | async-start | bytes 2097152 | tf_op jit(solution)/shard_map/all_to_all | solution.py:284
  224.1 0.8 fusion.9.lookup
  224.9 18.2 %all-to-all-done.2.ghosts = f32[128,4,4,128]{3,2,1,0:T(4,128)S(1)} async-done(((f32[128,4,4,128]{3,2,1,0:T(4,128)}), f32[128,4,4,128]{3,2,1,0:T(4,128)S(1)}, u32[]{:S(2)}, u32[]{:S(2)}) %all-to-all-start.2) | async-done | bytes 1048608 | tf_op jit(solution)/shard_map/all_to_all | solution.py:284
  243.1 1.0 copy-done
  244.1 50.6 %density.3 = (f32[128,128]{1,0:T(8,128)}, f32[128,4,128]{2,1,0:T(4,128)}, bf16[236,48,128]{2,1,0:T(8,128)(2,1)}, bf16[128,128,48]{2,1,0:T(8,128)(2,1)}, f32[236,8,128]{2,1,0:T(8,128)}) custom-call(s32[7]{0:T(128)} %stack.19.place, s32[128,16]{1,0:T(8,128)} %fusion.9.lookup, s32[128,4]{1,0:T(8,128)} %bitcast.7, f32[128,3,128]{2,1,0:T(4,128)} %get-tuple-element.28.points, ...), custom_call_target="tpu_custom_call" | custom-call | tf_op jit(solution)/shard_map/density/pallas_call | solution.py:295
  294.6 16.3 %all_to_all.20.rho_ghosts = f32[128,4,128]{2,1,0:T(4,128)} all-to-all(f32[128,4,128]{2,1,0:T(4,128)} %get-tuple-element.32), channel_id=1, replica_groups=mesh['gx'=4,'gy'=4,'gz'=8] {'gx','gy','gz'}, dimensions={0} | all-to-all | bytes 524288 | tf_op jit(solution)/shard_map/all_to_all | solution.py:284
  310.9 76.0 %last_force.1 = (f32[128,3,128]{2,1,0:T(4,128)}, f32[128,3,128]{2,1,0:T(4,128)}) custom-call(s32[7]{0:T(128)} %stack.19.place, s32[128,16]{1,0:T(8,128)} %fusion.9.lookup, f32[128,128]{1,0:T(8,128)} %get-tuple-element.47.rho, f32[128,4,128]{2,1,0:T(4,128)} %all_to_all.20.rho_ghosts, bf16[236,48,128]{2,1,0:T(8,128)(2,1)} %get-tuple-element.33.away_force, ...), custom_call_target="tpu_custom_call" | custom-call | tf_op jit(solution)/shard_map/last_force/pallas_call | solution.py:362
  386.9 1.6 copy.61
  388.6 1.6 copy.62
  (38 shorter events, 4.3 us)
Async XLA Ops:
  0.6 20.8 %copy-start.5 = (s32[128,16]{0,1:T(8,128)S(1)}, s32[128,16]{0,1:T(8,128)}, u32[]{:S(2)}) copy-start(s32[128,16]{0,1:T(8,128)} %param.12) | copy-start | bytes 24580
  0.6 94.5 %copy-start.3 = (f32[128,3,128]{2,0,1:T(8,128)S(1)}, f32[128,3,128]{2,0,1:T(8,128)}, u32[]{:S(2)}) copy-start(f32[128,3,128]{2,0,1:T(8,128)} %param.9) | copy-start | bytes 589828
  8.3 30.8 %all-to-all-start = ((f32[128,4,4,128]{3,2,1,0:T(4,128)}), f32[128,4,4,128]{3,2,1,0:T(4,128)S(1)}, u32[]{:S(2)}, u32[]{:S(2)}) async-start(f32[128,4,4,128]{3,2,1,0:T(4,128)} %pack.1), calls=%async_computation | async-start | bytes 2097152 | tf_op jit(solution)/shard_map/all_to_all | solution.py:284
  39.2 1.0 copy-start.1
  90.8 15.3 %all-to-all-start.1 = ((f32[128,4,128]{2,1,0:T(4,128)}), f32[128,4,128]{2,1,0:T(4,128)S(1)}, u32[]{:S(2)}, u32[]{:S(2)}) async-start(f32[128,4,128]{2,1,0:T(4,128)} %get-tuple-element.22), calls=%async_computation.1 | async-start | bytes 524288 | tf_op jit(solution)/shard_map/all_to_all | solution.py:284
  106.1 0.8 copy-start.2
  106.9 88.3 %copy-start.7 = (s32[1,128,4]{1,2,0:T(4,128)S(1)}, s32[1,128,4]{1,2,0:T(4,128)}, u32[]{:S(2)}) copy-start(s32[1,128,4]{1,2,0:T(4,128)} %param.14) | copy-start | bytes 6148
  106.9 116.8 %copy-start.6 = (s32[128,16]{0,1:T(8,128)S(1)}, s32[128,16]{0,1:T(8,128)}, u32[]{:S(2)}) copy-start(s32[128,16]{0,1:T(8,128)} %param.15) | copy-start | bytes 24580
  193.9 15.3 %collective-permute-start = (f32[2,8,128]{2,1,0:T(8,128)S(1)}, f32[2,8,128]{2,1,0:T(8,128)S(1)}, u32[]{:S(2)}, u32[]{:S(2)}) collective-permute-start(f32[2,8,128]{2,1,0:T(8,128)S(1)} %get-tuple-element.53), channel_id=1, source_target_pairs={{32,0},{64,32},{96,64},{33,1},{65,33},{97,65},{34,2},{66,34},{98,6... | collective-permute-start | bytes 24584 | tf_op jit(solution)/shard_map/ppermute | solution.py:290
  195.9 15.3 %collective-permute-start.1 = (f32[2,8,128]{2,1,0:T(8,128)S(1)}, f32[2,8,128]{2,1,0:T(8,128)S(1)}, u32[]{:S(2)}, u32[]{:S(2)}) collective-permute-start(f32[2,8,128]{2,1,0:T(8,128)S(1)} %get-tuple-element.52), channel_id=1, source_target_pairs={{0,32},{32,64},{64,96},{1,33},{33,65},{65,97},{2,34},{34,66},{66,9... | collective-permute-start | bytes 24584 | tf_op jit(solution)/shard_map/ppermute | solution.py:290
  199.9 11.3 %collective-permute-start.2 = (f32[2,8,128]{2,1,0:T(8,128)S(1)}, f32[2,8,128]{2,1,0:T(8,128)S(1)}, u32[]{:S(2)}, u32[]{:S(2)}) collective-permute-start(f32[2,8,128]{2,1,0:T(8,128)S(1)} %get-tuple-element.51), channel_id=1, source_target_pairs={{8,0},{16,8},{24,16},{9,1},{17,9},{25,17},{10,2},{18,10},{26,18},{... | collective-permute-start | bytes 24584 | tf_op jit(solution)/shard_map/ppermute | solution.py:290
  201.2 10.0 %collective-permute-start.3 = (f32[2,8,128]{2,1,0:T(8,128)S(1)}, f32[2,8,128]{2,1,0:T(8,128)S(1)}, u32[]{:S(2)}, u32[]{:S(2)}) collective-permute-start(f32[2,8,128]{2,1,0:T(8,128)S(1)} %get-tuple-element.50), channel_id=1, source_target_pairs={{0,8},{8,16},{16,24},{1,9},{9,17},{17,25},{2,10},{10,18},{18,26},{... | collective-permute-start | bytes 24584 | tf_op jit(solution)/shard_map/ppermute | solution.py:290
  205.2 6.1 %collective-permute-start.4 = (f32[2,8,128]{2,1,0:T(8,128)S(1)}, f32[2,8,128]{2,1,0:T(8,128)S(1)}, u32[]{:S(2)}, u32[]{:S(2)}) collective-permute-start(f32[2,8,128]{2,1,0:T(8,128)S(1)} %get-tuple-element.49), channel_id=1, source_target_pairs={{1,0},{2,1},{3,2},{4,3},{5,4},{6,5},{7,6},{9,8},{10,9},{11,10},{12... | collective-permute-start | bytes 24584 | tf_op jit(solution)/shard_map/ppermute | solution.py:290
  209.2 3.1 collective-permute-start.5
  212.3 0.8 copy-start.4
  218.1 24.9 %all-to-all-start.2 = ((f32[128,4,4,128]{3,2,1,0:T(4,128)}), f32[128,4,4,128]{3,2,1,0:T(4,128)S(1)}, u32[]{:S(2)}, u32[]{:S(2)}) async-start(f32[128,4,4,128]{3,2,1,0:T(4,128)} %get-tuple-element.30), calls=%async_computation.2 | async-start | bytes 2097152 | tf_op jit(solution)/shard_map/all_to_all | solution.py:284
  243.1 1.0 copy-start

commit v2 on v1

--- a/solution.py
+++ b/solution.py
@@ -27,7 +27,7 @@
     return jax.ShapeDtypeStruct(dims, dtype)
 
 
-def call(kernel, name, in_specs, out_shape, scratch=()):
+def call(kernel, name, in_specs, out_shape, scratch=(), cost=None):
     many = isinstance(out_shape, (list, tuple))
     return pl.pallas_call(
         kernel,
@@ -36,6 +36,7 @@
         out_shape=out_shape,
         scratch_shapes=list(scratch),
         compiler_params=pltpu.CompilerParams(vmem_limit_bytes=VMEM_LIMIT),
+        cost_estimate=cost and pl.CostEstimate(flops=cost[0], bytes_accessed=cost[1], transcendentals=0),
         name=name,
     )
 
@@ -94,13 +95,21 @@
     return jnp.sum(values.T, axis=0, keepdims=True)
 
 
-def density_kernel(place, lookup, send, points, mass, ghosts, rho, rho_send, away_force, home, local, away_density):
+def own_kernel(place, points, mass, away_density, away_force, home, local):
     def own(block, carry):
         rows = prepare(place, block, points[block], mass[pl.ds(block, 1)], away_density, away_force, local)
         home[block] = home_terms(rows).T.astype(bf16)
         return carry
 
-    lax.fori_loop(0, BLOCKS, own, 0)
+    lax.fori_loop(0, BLOCKS, own, 0, unroll=4)
+
+
+def density_kernel(
+    place, lookup, send, ghosts, own_density, own_force, home, own_local, rho, rho_send, away_force, local, away_density
+):
+    away_density[0:BLOCKS] = own_density[...]
+    away_force[0:BLOCKS] = own_force[...]
+    local[0:BLOCKS] = own_local[...]
 
     def other(code, carry):
         device = near_device(place, code)
@@ -109,9 +118,9 @@
             prepare(place, BLOCKS + code * GHOST_CAP + slot, block[0:3], block[3:4], away_density, away_force, local)
         return carry
 
-    lax.fori_loop(0, CODES, other, 0)
-
-    unroll = 4
+    lax.fori_loop(0, CODES, other, 0, unroll=3)
+
+    unroll = 8
 
     def some(step, carry):
         for part in range(unroll):
@@ -146,11 +155,9 @@
 
 
 def force_kernel(place, lookup, rho, rho_ghosts, away_force, home, local, emit):
-    def own(block, carry):
-        local[block, 3:4] = pressure(rho[pl.ds(block, 1)])
-        return carry
-
-    lax.fori_loop(0, BLOCKS, own, 0)
+    terms = pressure(rho[...])
+    for block in range(BLOCKS):
+        local[block, 3:4] = terms[block : block + 1]
 
     def other(code, carry):
         device = near_device(place, code)
@@ -159,9 +166,9 @@
             local[BLOCKS + code * GHOST_CAP + slot, 3:4] = values[slot : slot + 1]
         return carry
 
-    lax.fori_loop(0, CODES, other, 0)
-
-    unroll = 2
+    lax.fori_loop(0, CODES, other, 0, unroll=3)
+
+    unroll = 4
 
     def some(step, carry):
         for part in range(unroll):
@@ -189,44 +196,6 @@
     lax.fori_loop(0, BLOCKS // unroll, some, 0)
 
 
-def move_kernel(place, target, state, stay, outbox):
-    outbox[...] = jnp.zeros_like(outbox)
-
-    def one(block, counts):
-        goal = target[block]
-        device = goal // BLOCKS
-        spot = goal % BLOCKS
-        rows = state[block]
-        here = device == place[0]
-
-        @pl.when(here)
-        def _():
-            stay[spot] = rows
-
-        dx = device // (place[5] * place[6]) - place[1]
-        dy = device // place[6] % place[5] - place[2]
-        dz = device % place[6] - place[3]
-        heading = jnp.where(
-            dx != 0,
-            jnp.where(dx > 0, 1, 0),
-            jnp.where(dy != 0, jnp.where(dy > 0, 3, 2), jnp.where(dz > 0, 5, 4)),
-        )
-        used = counts[0]
-        for k in range(1, 6):
-            used = jnp.where(heading == k, counts[k], used)
-
-        @pl.when(jnp.logical_not(here))
-        def _():
-            slot = heading * MOVE_CAP + jnp.minimum(used, MOVE_CAP - 1)
-            outbox[slot, 0:7] = rows[0:7]
-            outbox[slot, 7:8] = jnp.full((1, WIDTH), spot + 1, jnp.int32).astype(f32)
-
-        gone = jnp.where(here, 0, 1)
-        return tuple(counts[k] + jnp.where(heading == k, gone, 0) for k in range(6))
-
-    lax.fori_loop(0, BLOCKS, one, (jnp.int32(0),) * 6)
-
-
 def merge_kernel(place, labels, send, stay, arrived, points, velocity, mass, ghost_send):
     def put(spot, rows):
         points[spot] = rows[0:3]
@@ -280,6 +249,27 @@
     return jnp.where(neighbours < BLOCKS, neighbours, BLOCKS + code * GHOST_CAP + within)
 
 
+def goals(destination):
+    size_y = lax.axis_size("gy")
+    size_z = lax.axis_size("gz")
+    device = destination // BLOCKS
+    place = destination % BLOCKS
+    moving = device != lax.axis_index(AXES)
+    dx = device // (size_y * size_z) - lax.axis_index("gx")
+    dy = device // size_z % size_y - lax.axis_index("gy")
+    dz = device % size_z - lax.axis_index("gz")
+    heading = jnp.where(
+        dx != 0,
+        (dx > 0).astype(jnp.int32),
+        jnp.where(dy != 0, 2 + (dy > 0).astype(jnp.int32), 4 + (dz > 0).astype(jnp.int32)),
+    )
+    heading = jnp.where(moving, heading, -1)
+    number = jnp.arange(BLOCKS, dtype=jnp.int32)
+    before = (heading[:, None] == heading[None, :]) & (number[None, :] < number[:, None])
+    used = jnp.minimum(jnp.sum(before.astype(jnp.int32), axis=1), MOVE_CAP - 1)
+    return jnp.where(moving, BLOCKS + heading * MOVE_CAP + used, place), place + 1
+
+
 def to_all(values):
     return lax.all_to_all(values, AXES, 0, 0, tiled=True)
 
@@ -292,19 +282,32 @@
 
 def densities(place, lookup, send, points, mass, ghost_send, devices):
     ghosts = to_all(ghost_send)
-    return call(
+    own_density, own_force, home, own_local = call(
+        own_kernel,
+        "own",
+        [SMEM] + [VMEM] * 2,
+        [
+            shape(BLOCKS, TERMS, WIDTH, dtype=bf16),
+            shape(BLOCKS, TERMS, WIDTH, dtype=bf16),
+            shape(BLOCKS, WIDTH, TERMS, dtype=bf16),
+            shape(BLOCKS, 8, WIDTH),
+        ],
+        cost=(10_000_000_000, 8_000_000),
+    )(place, points, mass)
+    rho, rho_send, away_force, local = call(
         density_kernel,
         "density",
-        [SMEM] * 3 + [VMEM] * 3,
+        [SMEM] * 3 + [VMEM] * 5,
         [
             shape(BLOCKS, WIDTH),
             shape(devices, GHOST_CAP, WIDTH),
             shape(STORED, TERMS, WIDTH, dtype=bf16),
-            shape(BLOCKS, WIDTH, TERMS, dtype=bf16),
             shape(STORED, 8, WIDTH),
         ],
         [pltpu.VMEM((STORED, TERMS, WIDTH), bf16)],
-    )(place, lookup, send, points, mass, ghosts)
+        cost=(80_000_000_000, 8_000_000),
+    )(place, lookup, send, ghosts, own_density, own_force, home, own_local)
+    return rho, rho_send, away_force, home, local
 
 
 def per_device(position, velocity, mass, send_first, neighbours_first, destination, send_second, neighbours_second):
@@ -324,26 +327,28 @@
     )
     rho_ghosts = to_all(rho_send)
 
-    def first(place, lookup, rho, rho_ghosts, away_force, home, local_in, points, velocity, mass, state, local):
+    slots, marks = goals(destination)
+
+    def first(place, lookup, slots, marks, rho, rho_ghosts, away_force, home, local_in, points, velocity, mass, state, local):
         local[...] = local_in[...]
+        state[BLOCKS:] = jnp.zeros((6 * MOVE_CAP, 8, WIDTH), f32)
 
         def emit(block, pull):
             speed = velocity[block] + time_step * pull
-            state[block, 0:3] = points[block] + time_step * speed
-            state[block, 3:6] = speed
-            state[block, 6:7] = mass[pl.ds(block, 1)]
+            mark = jnp.full((1, WIDTH), marks[block], jnp.int32).astype(f32)
+            rows = [points[block] + time_step * speed, speed, mass[pl.ds(block, 1)], mark]
+            state[slots[block]] = jnp.concatenate(rows, axis=0)
 
         force_kernel(place, lookup, rho, rho_ghosts, away_force, home, local, emit)
 
     state = call(
-        first, "force", [SMEM] * 2 + [VMEM] * 8, shape(BLOCKS, 8, WIDTH), [pltpu.VMEM((STORED, 8, WIDTH), f32)]
-    )(place, lookup_first, rho, rho_ghosts, away_force, home, local, position, velocity, mass)
-    stay, outbox = call(
-        move_kernel,
-        "move",
-        [SMEM] * 2 + [VMEM],
-        [shape(BLOCKS, 8, WIDTH), shape(6 * MOVE_CAP, 8, WIDTH)],
-    )(place, destination, state)
+        first,
+        "force",
+        [SMEM] * 4 + [VMEM] * 8,
+        shape(BLOCKS + 6 * MOVE_CAP, 8, WIDTH),
+        [pltpu.VMEM((STORED, 8, WIDTH), f32)],
+    )(place, lookup_first, slots, marks, rho, rho_ghosts, away_force, home, local, position, velocity, mass)
+    outbox = state[BLOCKS:]
     boxes = outbox.reshape(6, MOVE_CAP, 8, WIDTH)
     arrived = jnp.concatenate(
         [shifted(boxes[2 * k + way], axis, 2 * way - 1) for k, axis in enumerate(AXES) for way in (0, 1)], axis=0
@@ -354,7 +359,7 @@
         "merge",
         [SMEM] * 3 + [VMEM] * 2,
         [shape(BLOCKS, 3, WIDTH), shape(BLOCKS, 3, WIDTH), shape(BLOCKS, WIDTH), ghost_shape],
-    )(place, labels, send_second, stay, arrived)
+    )(place, labels, send_second, state, arrived)
     rho, rho_send, away_force, home, local = densities(
         place, lookup_second, send_second, position, mass, ghost_send, devices
     )

time: 391 us -> 327 us (0.84)
  Pallas kernels: 272 us -> 225 us
  waiting for transfers between devices: 46.1 us -> 29.3 us
    pallas_call x4 -> x5, Pallas kernels: 187 us -> 147 us  [the longest x1 69 us: per_device(): call(first, 'force', [SMEM] * 4 + [VMEM] * 8, shape(BLOCKS + 6 * MOVE_CAP...]
    all_to_all x3, waiting for transfers between devices: 45.1 us -> 28.3 us  [to_all(): return lax.all_to_all(values, AXES, 0, 0, tiled=True)]
    pallas_call x1, Pallas kernels: 76 us -> 68.9 us  [per_device(): call(last_force_kernel, 'last_force', [SMEM] * 2 + [VMEM] * 7, [shape(BLO...]
    unnamed x29 -> x31, local copies, waits for them, and re-layouts: 11.8 us -> 11 us
  transfers between devices with their start and end apart: 9 -> 9, of which waited for: 4 -> 4; matrix products, arithmetic and copies ran while one was open for 1% -> 2% of each run, Pallas kernels for 0% -> 5%
where the time goes in v2:
time: 327 us; the launch traced here: 326 us
  Pallas kernels  225 us (69%)
  starting transfers between devices  37.9 us (12%)
  waiting for transfers between devices  29.3 us (9%)
  blocking collectives  16.2 us (5%)
  local copies, waits for them, and re-layouts  12.9 us (4%)
  other arithmetic  3.78 us (1%)
    pallas_call x1, Pallas kernels, per_device(): call(first, 'force', [SMEM] * 4 + [VMEM] * 8, shape(BLOCKS + 6 * MOVE_CAP...  69 us
    pallas_call x1, Pallas kernels, per_device(): call(last_force_kernel, 'last_force', [SMEM] * 2 + [VMEM] * 7, [shape(BLO...  68.9 us
    pallas_call x2, Pallas kernels, densities(): call(density_kernel, 'density', [SMEM] * 3 + [VMEM] * 5, [shape(BLOCKS, W...  61.2 us
    all_to_all x3, waiting for transfers between devices, to_all(): return lax.all_to_all(values, AXES, 0, 0, tiled=True)  28.3 us
    all_to_all x3, starting transfers between devices, to_all(): return lax.all_to_all(values, AXES, 0, 0, tiled=True)  21.5 us
    pallas_call x2, Pallas kernels, densities(): call(own_kernel, 'own', [SMEM] + [VMEM] * 2, [shape(BLOCKS, TERMS, WIDTH,...  17.2 us
    ppermute x6, starting transfers between devices, shifted(): return lax.ppermute(values, axis, pairs)  16.5 us
    all_to_all x1, blocking collectives, to_all(): return lax.all_to_all(values, AXES, 0, 0, tiled=True)  16.2 us
  transfers between devices with their start and end apart: 9, of which 4 were waited for; matrix products, arithmetic and copies ran while one was open for 2% of the time, Pallas kernels for 5%

profile of v2, /device:TPU:1, one launch (start us, length us, event | category | flops | bytes accessed | tf_op | source)
XLA Modules:
  0.0 326.1 jit_solution(14766369927558808298)
XLA Ops:
  0.7 1.8 copy.75.points
  2.4 1.4 copy.74
  4.5 3.8 %pack.1 = f32[128,4,4,128]{3,2,1,0:T(4,128)} custom-call(s32[7]{0:T(128)} %stack.19.place, s32[128,4]{1,0:T(8,128)} %bitcast.8, f32[128,3,128]{2,1,0:T(4,128)} %copy.75.points, f32[128,128]{1,0:T(8,128)} %mass.5), custom_call_target="tpu_custom_call" | custom-call | tf_op jit(solution)/shard_map/pack/pallas_call | solution.py:324
  8.3 11.5 %all-to-all-start = ((f32[128,4,4,128]{3,2,1,0:T(4,128)}), f32[128,4,4,128]{3,2,1,0:T(4,128)S(1)}, u32[]{:S(2)}, u32[]{:S(2)}) async-start(f32[128,4,4,128]{3,2,1,0:T(4,128)} %pack.1), calls=%async_computation | async-start | bytes 2097152 | tf_op jit(solution)/shard_map/all_to_all | solution.py:274
  20.8 0.8 fusion.25.lookup
  21.8 8.6 %own.2 = (bf16[128,48,128]{2,1,0:T(8,128)(2,1)}, bf16[128,48,128]{2,1,0:T(8,128)(2,1)}, bf16[128,128,48]{2,1,0:T(8,128)(2,1)}, f32[128,8,128]{2,1,0:T(8,128)}) custom-call(s32[7]{0:T(128)} %stack.19.place, f32[128,3,128]{2,1,0:T(4,128)} %copy.75.points, f32[128,128]{1,0:T(8,128)} %mass.5), custom_call_target="tpu_custom_call" | custom-call | flops 10000000000 | bytes 8000000 | tf_op jit(solution)/shard_map/own/pallas_call | solution.py:285
  30.4 8.8 %all-to-all-done.ghosts = f32[128,4,4,128]{3,2,1,0:T(4,128)S(1)} async-done(((f32[128,4,4,128]{3,2,1,0:T(4,128)}), f32[128,4,4,128]{3,2,1,0:T(4,128)S(1)}, u32[]{:S(2)}, u32[]{:S(2)}) %all-to-all-start) | async-done | bytes 1048608 | tf_op jit(solution)/shard_map/all_to_all | solution.py:274
  39.2 1.0 copy-done.1
  40.2 30.6 %density.2 = (f32[128,128]{1,0:T(8,128)}, f32[128,4,128]{2,1,0:T(4,128)}, bf16[236,48,128]{2,1,0:T(8,128)(2,1)}, f32[236,8,128]{2,1,0:T(8,128)}) custom-call(s32[7]{0:T(128)} %stack.19.place, s32[128,16]{1,0:T(8,128)} %fusion.25.lookup, s32[128,4]{1,0:T(8,128)} %bitcast.9, f32[128,4,4,128]{3,2,1,0:T(4,128)} %copy-done.1, ...), custom_call_target="tpu_custom_call" | custom-call | flops 80000000000 | bytes 8000000 | tf_op jit(solution)/shard_map/density/pallas_call | solution.py:297
  70.8 4.3 %all-to-all-start.1 = ((f32[128,4,128]{2,1,0:T(4,128)}), f32[128,4,128]{2,1,0:T(4,128)S(1)}, u32[]{:S(2)}, u32[]{:S(2)}) async-start(f32[128,4,128]{2,1,0:T(4,128)} %get-tuple-element.30), calls=%async_computation.1 | async-start | bytes 524288 | tf_op jit(solution)/shard_map/all_to_all | solution.py:274
  75.7 0.8 copy.78.velocity
  76.5 9.6 %all-to-all-done.1.rho_ghosts = f32[128,4,128]{2,1,0:T(4,128)S(1)} async-done(((f32[128,4,128]{2,1,0:T(4,128)}), f32[128,4,128]{2,1,0:T(4,128)S(1)}, u32[]{:S(2)}, u32[]{:S(2)}) %all-to-all-start.1) | async-done | bytes 262176 | tf_op jit(solution)/shard_map/all_to_all | solution.py:274
  86.8 69.0 %force.1.stay = f32[140,8,128]{2,1,0:T(8,128)} custom-call(s32[7]{0:T(128)} %stack.19.place, s32[128,16]{1,0:T(8,128)} %fusion.25.lookup, s32[128]{0:T(128)} %compare_select_fusion.7.slots, s32[128]{0:T(128)} %get-tuple-element.59.marks, f32[128,128]{1,0:T(8,128)} %get-tuple-element.29.rho, f32[128,4,128]{2,1,0:T(4,128)} %copy-done, ...), custom_call_target="tpu_custom_call" | custom-call | tf_op jit(solution)/shard_map/force/pallas_call | solution.py:344
  156.6 1.3 collective-permute-start
  159.0 4.0 %collective-permute-start.1 = (f32[2,8,128]{2,1,0:T(8,128)S(1)}, f32[2,8,128]{2,1,0:T(8,128)S(1)}, u32[]{:S(2)}, u32[]{:S(2)}) collective-permute-start(f32[2,8,128]{2,1,0:T(8,128)S(1)} %get-tuple-element.67), channel_id=1, source_target_pairs={{0,32},{32,64},{64,96},{1,33},{33,65},{65,97},{2,34},{34,66},{66,9... | collective-permute-start | bytes 24584 | tf_op jit(solution)/shard_map/ppermute | solution.py:280
  163.0 1.3 collective-permute-start.2
  164.3 4.0 %collective-permute-start.3 = (f32[2,8,128]{2,1,0:T(8,128)S(1)}, f32[2,8,128]{2,1,0:T(8,128)S(1)}, u32[]{:S(2)}, u32[]{:S(2)}) collective-permute-start(f32[2,8,128]{2,1,0:T(8,128)S(1)} %get-tuple-element.65), channel_id=1, source_target_pairs={{0,8},{8,16},{16,24},{1,9},{9,17},{17,25},{2,10},{10,18},{18,26},{... | collective-permute-start | bytes 24584 | tf_op jit(solution)/shard_map/ppermute | solution.py:280
  168.3 3.9 %collective-permute-start.4 = (f32[2,8,128]{2,1,0:T(8,128)S(1)}, f32[2,8,128]{2,1,0:T(8,128)S(1)}, u32[]{:S(2)}, u32[]{:S(2)}) collective-permute-start(f32[2,8,128]{2,1,0:T(8,128)S(1)} %get-tuple-element.64), channel_id=1, source_target_pairs={{1,0},{2,1},{3,2},{4,3},{5,4},{6,5},{7,6},{9,8},{10,9},{11,10},{12... | collective-permute-start | bytes 24584 | tf_op jit(solution)/shard_map/ppermute | solution.py:280
  172.2 2.0 collective-permute-start.5
  174.3 0.9 collective-permute-done.5
  175.3 0.8 fusion.39.labels
  176.1 5.1 %merge.1 = (f32[128,3,128]{2,1,0:T(4,128)}, f32[128,3,128]{2,1,0:T(4,128)}, f32[128,128]{1,0:T(8,128)}, f32[128,4,4,128]{3,2,1,0:T(4,128)}) custom-call(s32[7]{0:T(128)} %stack.19.place, s32[12]{0:T(128)} %fusion.39.labels, s32[128,4]{1,0:T(8,128)} %bitcast.6, f32[140,8,128]{2,1,0:T(8,128)} %force.1.stay, f32[12,8,128]{2,1,0:T(8,128)} %copy-done.4), custom_call_target="tpu_custom_call" | custom-call | tf_op jit(solution)/shard_map/merge/pallas_call | solution.py:357
  181.2 5.6 %all-to-all-start.2 = ((f32[128,4,4,128]{3,2,1,0:T(4,128)}), f32[128,4,4,128]{3,2,1,0:T(4,128)S(1)}, u32[]{:S(2)}, u32[]{:S(2)}) async-start(f32[128,4,4,128]{3,2,1,0:T(4,128)} %get-tuple-element.33), calls=%async_computation.2 | async-start | bytes 2097152 | tf_op jit(solution)/shard_map/all_to_all | solution.py:274
  186.8 0.8 fusion.9.lookup
  187.7 8.6 %own.3 = (bf16[128,48,128]{2,1,0:T(8,128)(2,1)}, bf16[128,48,128]{2,1,0:T(8,128)(2,1)}, bf16[128,128,48]{2,1,0:T(8,128)(2,1)}, f32[128,8,128]{2,1,0:T(8,128)}) custom-call(s32[7]{0:T(128)} %stack.19.place, f32[128,3,128]{2,1,0:T(4,128)} %get-tuple-element.34.points, f32[128,128]{1,0:T(8,128)} %get-tuple-element.35.mass), custom_call_target="tpu_custom_call" | custom-call | flops 10000000000 | bytes 8000000 | tf_op jit(solution)/shard_map/own/pallas_call | solution.py:285
  196.3 9.9 %all-to-all-done.2.ghosts = f32[128,4,4,128]{3,2,1,0:T(4,128)S(1)} async-done(((f32[128,4,4,128]{3,2,1,0:T(4,128)}), f32[128,4,4,128]{3,2,1,0:T(4,128)S(1)}, u32[]{:S(2)}, u32[]{:S(2)}) %all-to-all-start.2) | async-done | bytes 1048608 | tf_op jit(solution)/shard_map/all_to_all | solution.py:274
  206.2 1.0 copy-done.2
  207.2 30.6 %density.3 = (f32[128,128]{1,0:T(8,128)}, f32[128,4,128]{2,1,0:T(4,128)}, bf16[236,48,128]{2,1,0:T(8,128)(2,1)}, f32[236,8,128]{2,1,0:T(8,128)}) custom-call(s32[7]{0:T(128)} %stack.19.place, s32[128,16]{1,0:T(8,128)} %fusion.9.lookup, s32[128,4]{1,0:T(8,128)} %bitcast.7, f32[128,4,4,128]{3,2,1,0:T(4,128)} %copy-done.2, ...), custom_call_target="tpu_custom_call" | custom-call | flops 80000000000 | bytes 8000000 | tf_op jit(solution)/shard_map/density/pallas_call | solution.py:297
  237.8 16.2 %all_to_all.20.rho_ghosts = f32[128,4,128]{2,1,0:T(4,128)} all-to-all(f32[128,4,128]{2,1,0:T(4,128)} %get-tuple-element.41), channel_id=1, replica_groups=mesh['gx'=4,'gy'=4,'gz'=8] {'gx','gy','gz'}, dimensions={0} | all-to-all | bytes 524288 | tf_op jit(solution)/shard_map/all_to_all | solution.py:274
  253.9 68.9 %last_force.1 = (f32[128,3,128]{2,1,0:T(4,128)}, f32[128,3,128]{2,1,0:T(4,128)}) custom-call(s32[7]{0:T(128)} %stack.19.place, s32[128,16]{1,0:T(8,128)} %fusion.9.lookup, f32[128,128]{1,0:T(8,128)} %get-tuple-element.58.rho, f32[128,4,128]{2,1,0:T(4,128)} %all_to_all.20.rho_ghosts, bf16[236,48,128]{2,1,0:T(8,128)(2,1)} %get-tuple-element.42.away_force, ...), custom_call_target="tpu_custom_call" | custom-call | tf_op jit(solution)/shard_map/last_force/pallas_call | solution.py:367
  322.8 1.6 copy.79
  324.5 1.6 copy.80
  (45 shorter events, 4.9 us)
Async XLA Ops:
  0.6 19.2 %copy-start.5 = (s32[128,16]{0,1:T(8,128)S(1)}, s32[128,16]{0,1:T(8,128)}, u32[]{:S(2)}) copy-start(s32[128,16]{0,1:T(8,128)} %param.12) | copy-start | bytes 24580
  0.6 19.6 %copy-start.8 = (s32[128]{0:T(128)S(1)}, s32[128]{0:T(128)}, u32[]{:S(2)}) copy-start(s32[128]{0:T(128)} %param.13) | copy-start | bytes 1540
  8.3 30.8 %all-to-all-start = ((f32[128,4,4,128]{3,2,1,0:T(4,128)}), f32[128,4,4,128]{3,2,1,0:T(4,128)S(1)}, u32[]{:S(2)}, u32[]{:S(2)}) async-start(f32[128,4,4,128]{3,2,1,0:T(4,128)} %pack.1), calls=%async_computation | async-start | bytes 2097152 | tf_op jit(solution)/shard_map/all_to_all | solution.py:274
  39.2 1.0 copy-start.1
  40.2 35.5 %copy-start.3 = (f32[128,3,128]{2,0,1:T(8,128)S(1)}, f32[128,3,128]{2,0,1:T(8,128)}, u32[]{:S(2)}) copy-start(f32[128,3,128]{2,0,1:T(8,128)} %param.9) | copy-start | bytes 589828
  40.2 36.4 %copy-start.6 = (s32[128,16]{0,1:T(8,128)S(1)}, s32[128,16]{0,1:T(8,128)}, u32[]{:S(2)}) copy-start(s32[128,16]{0,1:T(8,128)} %param.15) | copy-start | bytes 24580
  70.8 15.3 %all-to-all-start.1 = ((f32[128,4,128]{2,1,0:T(4,128)}), f32[128,4,128]{2,1,0:T(4,128)S(1)}, u32[]{:S(2)}, u32[]{:S(2)}) async-start(f32[128,4,128]{2,1,0:T(4,128)} %get-tuple-element.30), calls=%async_computation.1 | async-start | bytes 524288 | tf_op jit(solution)/shard_map/all_to_all | solution.py:274
  86.1 0.7 copy-start
  86.8 71.2 %copy-start.7 = (s32[1,128,4]{1,2,0:T(4,128)S(1)}, s32[1,128,4]{1,2,0:T(4,128)}, u32[]{:S(2)}) copy-start(s32[1,128,4]{1,2,0:T(4,128)} %param.14) | copy-start | bytes 6148
  156.6 15.6 %collective-permute-start = (f32[2,8,128]{2,1,0:T(8,128)S(1)}, f32[2,8,128]{2,1,0:T(8,128)S(1)}, u32[]{:S(2)}, u32[]{:S(2)}) collective-permute-start(f32[2,8,128]{2,1,0:T(8,128)S(1)} %get-tuple-element.68), channel_id=1, source_target_pairs={{32,0},{64,32},{96,64},{33,1},{65,33},{97,65},{34,2},{66,34},{98,6... | collective-permute-start | bytes 24584 | tf_op jit(solution)/shard_map/ppermute | solution.py:280
  159.0 15.2 %collective-permute-start.1 = (f32[2,8,128]{2,1,0:T(8,128)S(1)}, f32[2,8,128]{2,1,0:T(8,128)S(1)}, u32[]{:S(2)}, u32[]{:S(2)}) collective-permute-start(f32[2,8,128]{2,1,0:T(8,128)S(1)} %get-tuple-element.67), channel_id=1, source_target_pairs={{0,32},{32,64},{64,96},{1,33},{33,65},{65,97},{2,34},{34,66},{66,9... | collective-permute-start | bytes 24584 | tf_op jit(solution)/shard_map/ppermute | solution.py:280
  163.0 11.3 %collective-permute-start.2 = (f32[2,8,128]{2,1,0:T(8,128)S(1)}, f32[2,8,128]{2,1,0:T(8,128)S(1)}, u32[]{:S(2)}, u32[]{:S(2)}) collective-permute-start(f32[2,8,128]{2,1,0:T(8,128)S(1)} %get-tuple-element.66), channel_id=1, source_target_pairs={{8,0},{16,8},{24,16},{9,1},{17,9},{25,17},{10,2},{18,10},{26,18},{... | collective-permute-start | bytes 24584 | tf_op jit(solution)/shard_map/ppermute | solution.py:280
  164.3 10.0 %collective-permute-start.3 = (f32[2,8,128]{2,1,0:T(8,128)S(1)}, f32[2,8,128]{2,1,0:T(8,128)S(1)}, u32[]{:S(2)}, u32[]{:S(2)}) collective-permute-start(f32[2,8,128]{2,1,0:T(8,128)S(1)} %get-tuple-element.65), channel_id=1, source_target_pairs={{0,8},{8,16},{16,24},{1,9},{9,17},{17,25},{2,10},{10,18},{18,26},{... | collective-permute-start | bytes 24584 | tf_op jit(solution)/shard_map/ppermute | solution.py:280
  168.3 6.0 %collective-permute-start.4 = (f32[2,8,128]{2,1,0:T(8,128)S(1)}, f32[2,8,128]{2,1,0:T(8,128)S(1)}, u32[]{:S(2)}, u32[]{:S(2)}) collective-permute-start(f32[2,8,128]{2,1,0:T(8,128)S(1)} %get-tuple-element.64), channel_id=1, source_target_pairs={{1,0},{2,1},{3,2},{4,3},{5,4},{6,5},{7,6},{9,8},{10,9},{11,10},{12... | collective-permute-start | bytes 24584 | tf_op jit(solution)/shard_map/ppermute | solution.py:280
  172.2 3.1 collective-permute-start.5
  175.3 0.9 copy-start.4
  181.2 25.0 %all-to-all-start.2 = ((f32[128,4,4,128]{3,2,1,0:T(4,128)}), f32[128,4,4,128]{3,2,1,0:T(4,128)S(1)}, u32[]{:S(2)}, u32[]{:S(2)}) async-start(f32[128,4,4,128]{3,2,1,0:T(4,128)} %get-tuple-element.33), calls=%async_computation.2 | async-start | bytes 2097152 | tf_op jit(solution)/shard_map/all_to_all | solution.py:274
  206.2 1.0 copy-start.2
